TPU v7x, 32 devices: a whole 2x2x4 slice. The times are simulated.
32 devices in a mesh: shard: 8 (over z, y), ctx: 2 (over x), tp: 2 (over core).
Axes of the slice: x: 2, y: 2, z: 4, core: 2. Of those that a mesh axis runs over, the one named last changes fastest.
Arguments:
- inputs: bfloat16 [2, 8192, 1024], P(None, ('shard', 'ctx')), may hold values from -6 to 6
- cotangent: bfloat16 [2, 8192, 1024], P(None, ('shard', 'ctx')), may hold values from -6 to 6
- lengths: int32 [2, 8], P(None, 'shard'), may hold values from 256 to 1024, as said below
- buckets: int32 [1024, 1024], P('ctx'), may hold values from 0 to 31, as said below
- query_weight: bfloat16 [1024, 1024], P(('shard', 'ctx'), 'tp'), may hold values from -0.09375 to 0.09375
- key_weight: bfloat16 [1024, 1024], P(('shard', 'ctx'), 'tp'), may hold values from -0.09375 to 0.09375
- value_weight: bfloat16 [1024, 1024], P(('shard', 'ctx'), 'tp'), may hold values from -0.1875 to 0.1875
- projection_weight: bfloat16 [1024, 1024], P(('shard', 'ctx'), 'tp'), may hold values from -1 to 1
- gate_weight: bfloat16 [1024, 2816], P(('shard', 'ctx'), 'tp'), may hold values from -0.1875 to 0.1875
- up_weight: bfloat16 [1024, 2816], P(('shard', 'ctx'), 'tp'), may hold values from -0.1875 to 0.1875
- down_weight: bfloat16 [1024, 2816], P(('shard', 'ctx'), 'tp'), may hold values from -0.21875 to 0.21875
- attention_gain: bfloat16 [1024], P(('shard', 'ctx')), may hold values from 0.099609375 to 1.8984375
- feedforward_gain: bfloat16 [1024], P(('shard', 'ctx')), may hold values from 0.099609375 to 1.8984375
- bias_table: bfloat16 [32, 16], P(None, 'tp'), may hold values from -4 to 4
Outputs:
- output: bfloat16 [2, 8192, 1024], P(None, ('shard', 'ctx'))
- input_grad: float32 [2, 8192, 1024], P(None, ('shard', 'ctx'))
- query_grad: float32 [1024, 1024], P(('shard', 'ctx'), 'tp')
- key_grad: float32 [1024, 1024], P(('shard', 'ctx'), 'tp')
- value_grad: float32 [1024, 1024], P(('shard', 'ctx'), 'tp')
- projection_grad: float32 [1024, 1024], P(('shard', 'ctx'), 'tp')
- gate_grad: float32 [1024, 2816], P(('shard', 'ctx'), 'tp')
- up_grad: float32 [1024, 2816], P(('shard', 'ctx'), 'tp')
- down_grad: float32 [1024, 2816], P(('shard', 'ctx'), 'tp')
- attention_gain_grad: float32 [1024], P(('shard', 'ctx'))
- feedforward_gain_grad: float32 [1024], P(('shard', 'ctx'))
- table_grad: float32 [32, 16], P(None, 'tp')
Inputs may be any that keep to these rules, and one draw needn't show every extreme that they name: For every sequence index s, at least one of the 2 micro-batches has lengths[m, s] = 1024. T5's bidirectional bucket (16 buckets each way, exact below a distance of 8, logarithmic up to 128) of key position minus query position, where the position ids rise by 1 or 2 from slot to slot.
All inputs are finite; a program needn't handle non-finite values.
Results may differ from a plain program's by a relative error of at most 0.017.
The roundings to bfloat16 on the way count: a program that leaves them out, or rounds other values in their place, can miss the bound.
Values may be sent and summed in bfloat16 or wider, within the bound.
A program may use at most 256 MiB of HBM per device.

v0:
```python
import math

import jax
import jax.numpy as jnp
from jax import lax
from jax.sharding import PartitionSpec as P

EPSILON = 1e-06
GELU_ROOT = 0.7978845608028654
GELU_CUBIC = 0.044715


def gelu_tanh(activation):
    return (
        0.5
        * activation
        * (
            1.0
            + jnp.tanh(GELU_ROOT * (activation + GELU_CUBIC * activation * activation * activation))
        )
    )


def gelu_slope(activation):
    tangent = jnp.tanh(GELU_ROOT * (activation + GELU_CUBIC * activation * activation * activation))
    return 0.5 * (1.0 + tangent) + 0.5 * activation * (1.0 - tangent * tangent) * GELU_ROOT * (
        1.0 + 3.0 * GELU_CUBIC * activation * activation
    )


def normalize(tokens_in, gain_values):
    inverse_norm = lax.rsqrt(jnp.mean(tokens_in * tokens_in, axis=-1, keepdims=True) + EPSILON)
    normal = tokens_in * inverse_norm
    return (normal, inverse_norm, (normal * gain_values).astype(jnp.bfloat16))


def normalize_back(grad_normed, normal, inverse_norm, gain_values):
    grad_normal = grad_normed * gain_values
    grad_tokens = inverse_norm * (
        grad_normal - normal * jnp.mean(grad_normal * normal, axis=-1, keepdims=True)
    )
    return (grad_tokens, jnp.sum(grad_normed * normal, axis=0))


def times_transposed(activations, weight):
    return lax.dot_general(
        activations, weight, (((1,), (1,)), ((), ())), preferred_element_type=jnp.float32
    )


def weight_gradient(activations, gradient_rows):
    return lax.dot_general(
        gradient_rows, activations, (((0,), (0,)), ((), ())), preferred_element_type=jnp.float32
    )


def bucket_blocks(buckets):
    row_count = buckets.shape[0]
    block_size = math.gcd(row_count, 256)
    return buckets.reshape(row_count // block_size, block_size, buckets.shape[1])


def bucket_onehot(bucket_block, bucket_count):
    return (bucket_block[None] == jnp.arange(bucket_count, dtype=jnp.int32)[:, None, None]).astype(
        jnp.bfloat16
    )


def bias_from(buckets, bias_table):
    bucket_count, head_count = bias_table.shape
    bucket_rows = bucket_blocks(buckets)

    def one_block(bucket_block):
        return jnp.einsum(
            "ngo,ns->sgo",
            bucket_onehot(bucket_block, bucket_count),
            bias_table,
            preferred_element_type=jnp.float32,
        )

    parts = lax.map(one_block, bucket_rows)
    return jnp.transpose(parts, (1, 0, 2, 3)).reshape(
        head_count, buckets.shape[0], buckets.shape[1]
    )


def table_from(buckets, grad_scores, bucket_count):
    bucket_rows = bucket_blocks(buckets)
    head_count = grad_scores.shape[0]
    grad_blocks = jnp.transpose(
        grad_scores.reshape(
            head_count, bucket_rows.shape[0], bucket_rows.shape[1], bucket_rows.shape[2]
        ),
        (1, 0, 2, 3),
    )

    def add_block(running, packed):
        bucket_block, grad_piece = packed
        return (
            running
            + jnp.einsum(
                "fkm,pkm->fp",
                bucket_onehot(bucket_block, bucket_count),
                grad_piece,
                preferred_element_type=jnp.float32,
            ),
            None,
        )

    running, _ = lax.scan(
        add_block, jnp.zeros((bucket_count, head_count), jnp.float32), (bucket_rows, grad_blocks)
    )
    return running


def shards(
    inputs,
    cotangent,
    lengths,
    buckets,
    query_weight,
    key_weight,
    value_weight,
    projection_weight,
    gate_weight,
    up_weight,
    down_weight,
    attention_gain,
    feedforward_gain,
    bias_table,
):
    bucket_count, head_count = bias_table.shape
    row_count = inputs.shape[1]
    head_size = query_weight.shape[1] // head_count
    key_count = row_count * lax.axis_size("ctx")
    first_row = lax.axis_index("ctx") * row_count
    query_place = first_row + jnp.arange(row_count, dtype=jnp.int32)
    key_place = jnp.arange(key_count, dtype=jnp.int32)
    bias_values = bias_from(buckets, bias_table)
    weight_shards = (
        query_weight,
        key_weight,
        value_weight,
        projection_weight,
        gate_weight,
        up_weight,
        down_weight,
        attention_gain,
        feedforward_gain,
    )
    spread = lax.axis_size(("shard", "ctx"))

    def scores_of(query_heads, key_heads, length):
        scores = (
            jnp.einsum("qhd,khd->hqk", query_heads, key_heads, preferred_element_type=jnp.float32)
            + bias_values
        )
        return jnp.where((key_place < length)[None, None, :], scores, -1e30)

    def forward_pass(gathered, tokens_in, length):
        (
            query_full,
            key_full,
            value_full,
            project_full,
            gate_full,
            up_full,
            down_full,
            gain_attention,
            gain_feedforward,
        ) = gathered
        present = tokens_in.astype(jnp.float32)
        normal_one, inverse_one, normed_one = normalize(present, gain_attention.astype(jnp.float32))
        queries = jnp.dot(normed_one, query_full, preferred_element_type=jnp.float32).astype(
            jnp.bfloat16
        )
        key_local = jnp.dot(normed_one, key_full, preferred_element_type=jnp.float32).astype(
            jnp.bfloat16
        )
        value_local = jnp.dot(normed_one, value_full, preferred_element_type=jnp.float32).astype(
            jnp.bfloat16
        )
        key_rows, value_rows = (
            lax.all_gather(key_local, "ctx", axis=0, tiled=True),
            lax.all_gather(value_local, "ctx", axis=0, tiled=True),
        )
        scores = scores_of(
            queries.reshape(row_count, head_count, head_size),
            key_rows.reshape(key_count, head_count, head_size),
            length,
        )
        highest = jnp.max(scores, axis=-1, keepdims=True)
        exponent = jnp.exp(scores - highest)
        row_total = jnp.sum(exponent, axis=-1, keepdims=True)
        attention_probs = (exponent / row_total).astype(jnp.bfloat16)
        log_total = highest + jnp.log(row_total)
        attended = jnp.einsum(
            "hqk,khd->qhd",
            attention_probs,
            value_rows.reshape(key_count, head_count, head_size),
            preferred_element_type=jnp.float32,
        )
        attended = attended.reshape(row_count, head_count * head_size).astype(jnp.bfloat16)
        branch = lax.psum(times_transposed(attended, project_full), "tp")
        middle = present + branch
        normal_two, inverse_two, normed_two = normalize(
            middle, gain_feedforward.astype(jnp.float32)
        )
        gate_value = jnp.dot(normed_two, gate_full, preferred_element_type=jnp.float32)
        up_value = jnp.dot(normed_two, up_full, preferred_element_type=jnp.float32)
        hidden = (gelu_tanh(gate_value) * up_value).astype(jnp.bfloat16)
        output = middle + lax.psum(times_transposed(hidden, down_full), "tp")
        saved = (
            normal_one,
            inverse_one,
            normed_one,
            queries,
            key_rows,
            value_rows,
            log_total,
            attended,
            normal_two,
            inverse_two,
            normed_two,
            gate_value,
            up_value,
            hidden,
        )
        return (output, saved)

    def backward_pass(gathered, saved, cot_rows, length):
        (
            query_full,
            key_full,
            value_full,
            project_full,
            gate_full,
            up_full,
            down_full,
            gain_attention,
            gain_feedforward,
        ) = gathered
        (
            normal_one,
            inverse_one,
            normed_one,
            queries,
            key_rows,
            value_rows,
            log_total,
            attended,
            normal_two,
            inverse_two,
            normed_two,
            gate_value,
            up_value,
            hidden,
        ) = saved
        live_rows = (query_place < length).astype(jnp.float32)[:, None]
        grad_out = cot_rows.astype(jnp.float32) * live_rows
        grad_low = grad_out.astype(jnp.bfloat16)
        grad_down = weight_gradient(hidden, grad_low)
        grad_hidden = jnp.dot(grad_low, down_full, preferred_element_type=jnp.float32)
        grad_gate = (grad_hidden * up_value * gelu_slope(gate_value)).astype(jnp.bfloat16)
        grad_up = (grad_hidden * gelu_tanh(gate_value)).astype(jnp.bfloat16)
        grad_gate_weight = weight_gradient(grad_gate, normed_two)
        grad_up_weight = weight_gradient(grad_up, normed_two)
        grad_two = lax.psum(
            times_transposed(grad_gate, gate_full) + times_transposed(grad_up, up_full), "tp"
        )
        grad_middle, grad_gain_feedforward = normalize_back(
            grad_two, normal_two, inverse_two, gain_feedforward.astype(jnp.float32)
        )
        grad_middle = grad_middle + grad_out
        grad_branch = grad_middle.astype(jnp.bfloat16)
        grad_project = weight_gradient(attended, grad_branch)
        grad_attended = jnp.dot(
            grad_branch, project_full, preferred_element_type=jnp.float32
        ).astype(jnp.bfloat16)
        grad_attended = grad_attended.reshape(row_count, head_count, head_size)
        query_heads = queries.reshape(row_count, head_count, head_size)
        key_heads = key_rows.reshape(key_count, head_count, head_size)
        value_heads = value_rows.reshape(key_count, head_count, head_size)
        scores = scores_of(query_heads, key_heads, length)
        soft = jnp.exp(scores - log_total)
        attention_probs = soft.astype(jnp.bfloat16)
        grad_values_part = jnp.einsum(
            "hqk,qhd->khd", attention_probs, grad_attended, preferred_element_type=jnp.float32
        )
        grad_probs = jnp.einsum(
            "qhd,khd->hqk", grad_attended, value_heads, preferred_element_type=jnp.float32
        )
        grad_scores = (
            soft * (grad_probs - jnp.sum(soft * grad_probs, axis=-1, keepdims=True))
        ).astype(jnp.bfloat16)
        grad_queries = jnp.einsum(
            "hqk,khd->qhd", grad_scores, key_heads, preferred_element_type=jnp.float32
        )
        grad_queries = grad_queries.reshape(row_count, head_count * head_size).astype(jnp.bfloat16)
        grad_keys_part = jnp.einsum(
            "hqk,qhd->khd", grad_scores, query_heads, preferred_element_type=jnp.float32
        )
        grad_keys, grad_values = (
            lax.psum_scatter(
                grad_keys_part.reshape(key_count, head_count * head_size),
                "ctx",
                scatter_dimension=0,
                tiled=True,
            ),
            lax.psum_scatter(
                grad_values_part.reshape(key_count, head_count * head_size),
                "ctx",
                scatter_dimension=0,
                tiled=True,
            ),
        )
        grad_keys = grad_keys.astype(jnp.bfloat16)
        grad_values = grad_values.astype(jnp.bfloat16)
        table_part = table_from(buckets, grad_scores, bucket_count)
        grad_query_weight = weight_gradient(grad_queries, normed_one)
        grad_key_weight = weight_gradient(grad_keys, normed_one)
        grad_value_weight = weight_gradient(grad_values, normed_one)
        grad_one = lax.psum(
            times_transposed(grad_queries, query_full)
            + times_transposed(grad_keys, key_full)
            + times_transposed(grad_values, value_full),
            "tp",
        )
        grad_present, grad_gain_attention = normalize_back(
            grad_one, normal_one, inverse_one, gain_attention.astype(jnp.float32)
        )
        grad_tokens = grad_present + grad_middle
        gradients = (
            grad_query_weight,
            grad_key_weight,
            grad_value_weight,
            grad_project,
            grad_gate_weight,
            grad_up_weight,
            grad_down,
            grad_gain_attention,
            grad_gain_feedforward,
        )
        return (grad_tokens, gradients, table_part)

    def micro_step(running_sums, micro_item):
        grad_running, table_running = running_sums
        tokens_in, cot_rows, length = micro_item
        gathered = (
            lax.all_gather(query_weight, ("shard", "ctx"), axis=0, tiled=True),
            lax.all_gather(key_weight, ("shard", "ctx"), axis=0, tiled=True),
            lax.all_gather(value_weight, ("shard", "ctx"), axis=0, tiled=True),
            lax.all_gather(projection_weight, ("shard", "ctx"), axis=0, tiled=True),
            lax.all_gather(gate_weight, ("shard", "ctx"), axis=0, tiled=True),
            lax.all_gather(up_weight, ("shard", "ctx"), axis=0, tiled=True),
            lax.all_gather(down_weight, ("shard", "ctx"), axis=0, tiled=True),
            lax.all_gather(attention_gain, ("shard", "ctx"), axis=0, tiled=True),
            lax.all_gather(feedforward_gain, ("shard", "ctx"), axis=0, tiled=True),
        )
        output, saved = forward_pass(gathered, tokens_in, length)
        gathered = (
            lax.all_gather(query_weight, ("shard", "ctx"), axis=0, tiled=True),
            lax.all_gather(key_weight, ("shard", "ctx"), axis=0, tiled=True),
            lax.all_gather(value_weight, ("shard", "ctx"), axis=0, tiled=True),
            lax.all_gather(projection_weight, ("shard", "ctx"), axis=0, tiled=True),
            lax.all_gather(gate_weight, ("shard", "ctx"), axis=0, tiled=True),
            lax.all_gather(up_weight, ("shard", "ctx"), axis=0, tiled=True),
            lax.all_gather(down_weight, ("shard", "ctx"), axis=0, tiled=True),
            lax.all_gather(attention_gain, ("shard", "ctx"), axis=0, tiled=True),
            lax.all_gather(feedforward_gain, ("shard", "ctx"), axis=0, tiled=True),
        )
        grad_tokens, gradients, table_part = backward_pass(gathered, saved, cot_rows, length)
        grad_running = tuple((first + second for first, second in zip(grad_running, gradients)))
        return (
            (grad_running, table_running + table_part),
            (output.astype(jnp.bfloat16), grad_tokens),
        )

    starting = tuple(
        (
            jnp.zeros((weight.shape[0] * spread,) + weight.shape[1:], jnp.float32)
            for weight in weight_shards
        )
    )
    table_start = jnp.zeros((bucket_count, head_count), jnp.float32)
    (grad_sums, table_running), (outputs, grad_inputs) = lax.scan(
        micro_step, (starting, table_start), (inputs, cotangent, lengths[:, 0])
    )
    finished = (
        lax.psum_scatter(grad_sums[0], ("shard", "ctx"), scatter_dimension=0, tiled=True),
        lax.psum_scatter(grad_sums[1], ("shard", "ctx"), scatter_dimension=0, tiled=True),
        lax.psum_scatter(grad_sums[2], ("shard", "ctx"), scatter_dimension=0, tiled=True),
        lax.psum_scatter(grad_sums[3], ("shard", "ctx"), scatter_dimension=0, tiled=True),
        lax.psum_scatter(grad_sums[4], ("shard", "ctx"), scatter_dimension=0, tiled=True),
        lax.psum_scatter(grad_sums[5], ("shard", "ctx"), scatter_dimension=0, tiled=True),
        lax.psum_scatter(grad_sums[6], ("shard", "ctx"), scatter_dimension=0, tiled=True),
        lax.psum_scatter(grad_sums[7], ("shard", "ctx"), scatter_dimension=0, tiled=True),
        lax.psum_scatter(grad_sums[8], ("shard", "ctx"), scatter_dimension=0, tiled=True),
    )
    table_total = lax.psum(table_running, ("shard", "ctx"))
    return (
        outputs,
        grad_inputs,
        finished[0],
        finished[1],
        finished[2],
        finished[3],
        finished[4],
        finished[5],
        finished[6],
        finished[7],
        finished[8],
        table_total,
    )


def solution(mesh):
    placed = (
        P(None, ("shard", "ctx"), None),
        P(None, ("shard", "ctx"), None),
        P(None, "shard"),
        P("ctx", None),
        P(("shard", "ctx"), "tp"),
        P(("shard", "ctx"), "tp"),
        P(("shard", "ctx"), "tp"),
        P(("shard", "ctx"), "tp"),
        P(("shard", "ctx"), "tp"),
        P(("shard", "ctx"), "tp"),
        P(("shard", "ctx"), "tp"),
        P(("shard", "ctx")),
        P(("shard", "ctx")),
        P(None, "tp"),
    )
    return jax.shard_map(
        shards,
        mesh=mesh,
        in_specs=placed,
        out_specs=(
            P(None, ("shard", "ctx"), None),
            P(None, ("shard", "ctx"), None),
            P(("shard", "ctx"), "tp"),
            P(("shard", "ctx"), "tp"),
            P(("shard", "ctx"), "tp"),
            P(("shard", "ctx"), "tp"),
            P(("shard", "ctx"), "tp"),
            P(("shard", "ctx"), "tp"),
            P(("shard", "ctx"), "tp"),
            P(("shard", "ctx")),
            P(("shard", "ctx")),
            P(None, "tp"),
        ),
        check_vma=False,
    )
```

profile of v0, /device:TPU:0, one launch (start us, length us, event | category | flops | bytes accessed | tf_op | source)
XLA Modules:
  0.0 2191.8 jit_solution(15223140841785906809)
XLA Ops:
  8.1 17.1 while.55
  25.2 17.8 copy.39
  43.1 1429.0 %while.57 = (s32[]{:T(128)}, f32[1024,512]{1,0:T(8,128)}, f32[1024,512]{1,0:T(8,128)}, f32[1024,512]{1,0:T(8,128)}, f32[1024,512]{1,0:T(8,128)}, /*index=5*/f32[...) while((s32[]{:T(128)}, f32[1024,512]{1,0:T(8,128)}, ...), condition=%wide.region_20.21_spmd.clone, body=%wide.region_2.20_spmd.clone.sunk | while | flops 23240048640 | bytes 887587392 | solution.py:386
  47.3 43.5 %all-reduce.11 = (bf16[1024]{0:T(1024)(128)(2,1)S(1)}, bf16[1024]{0:T(1024)(128)(2,1)S(1)}) all-reduce(bf16[1024]{0:T(1024)(128)(2,1)S(1)} %dynamic-update-slice.6, bf16[1024]{0:T(1024)(128)(2,1)S(1)} %dynamic-update-slice.7), channel_id=1, replica_groups=mesh['shard'=8,'ctx'=2,'tp'=2] {'shard','ctx'}, use_global_device_ids=true, to_apply=%add | all-reduce | flops 2048 | bytes 8192 | tf_op jit(solution)/shard_map/while
  91.1 13.9 all-gather.10.cloned.1.call-done
  107.9 54.0 %all-gather.18.cloned.1.call-done = bf16[1024,512]{1,0:T(8,128)(2,1)} async-done(((bf16[64,512]{1,0:T(8,128)(2,1)}), bf16[1024,512]{1,0:T(8,128)(2,1)}) %all-gather.18.cloned.1.call-update) | async-done | bytes 1048592 | tf_op jit(solution)/shard_map/while/body/eval_jaxpr/all_gather | solution.py:352
  166.6 52.2 %all-gather.14.cloned.1.call-done = bf16[1024,512]{1,0:T(8,128)(2,1)} async-done(((bf16[64,512]{1,0:T(8,128)(2,1)}), bf16[1024,512]{1,0:T(8,128)(2,1)}) %all-gather.14.cloned.1.call-update) | async-done | bytes 1048592 | tf_op jit(solution)/shard_map/while/body/eval_jaxpr/all_gather | solution.py:350
  221.7 18.7 all-gather.12.cloned.1.call-done
  241.8 8.7 fusion.253
  272.5 48.6 %all-gather.16.cloned.1.call-done = bf16[1024,512]{1,0:T(8,128)(2,1)} async-done(((bf16[64,512]{1,0:T(8,128)(2,1)}), bf16[1024,512]{1,0:T(8,128)(2,1)}) %all-gather.16.cloned.1.call-update) | async-done | bytes 1048592 | tf_op jit(solution)/shard_map/while/body/eval_jaxpr/all_gather | solution.py:353
  327.5 17.1 all-reduce.17.cloned.1.call-done
  348.0 66.8 %all-gather.24.cloned.1.call-done = bf16[1024,1408]{1,0:T(8,128)(2,1)} async-done(((bf16[64,1408]{1,0:T(8,128)(2,1)}), bf16[1024,1408]{1,0:T(8,128)(2,1)}) %all-gather.24.cloned.1.call-update) | async-done | bytes 2883600 | tf_op jit(solution)/shard_map/while/body/eval_jaxpr/all_gather | solution.py:368
  420.4 62.6 %all-gather.22.cloned.1.call-done = bf16[1024,1408]{1,0:T(8,128)(2,1)} async-done(((bf16[64,1408]{1,0:T(8,128)(2,1)}), bf16[1024,1408]{1,0:T(8,128)(2,1)}) %all-gather.22.cloned.1.call-update) | async-done | bytes 2883600 | tf_op jit(solution)/shard_map/while/body/eval_jaxpr/all_gather | solution.py:354
  488.5 62.4 %all-gather.26.cloned.1.call-done = bf16[1024,1408]{1,0:T(8,128)(2,1)} async-done(((bf16[64,1408]{1,0:T(8,128)(2,1)}), bf16[1024,1408]{1,0:T(8,128)(2,1)}) %all-gather.26.cloned.1.call-update) | async-done | bytes 2883600 | tf_op jit(solution)/shard_map/while/body/eval_jaxpr/all_gather | solution.py:355
  550.9 8.5 multiply_convert_fusion.8
  566.0 19.9 all-reduce.19.cloned.1.call-done
  591.6 14.7 multiply_reduce_fusion.9
  620.0 8.6 fusion.263
  643.5 9.6 reduce-scatter.24.cloned.1.call-done
  656.7 30.6 %reduce-scatter.26.cloned.1.call-done = f32[512,512]{0,1:T(8,128)} async-done(((f32[1024,512]{0,1:T(8,128)}), f32[512,512]{0,1:T(8,128)}) %reduce-scatter.26.cloned.1.call-update) | async-done | bytes 1048592 | tf_op jit(solution)/shard_map/while/body/eval_jaxpr/reduce_scatter | solution.py:310
  703.3 12.1 copy.47
  716.0 17.4 while.58
  759.2 41.2 %all-reduce.11 = (bf16[1024]{0:T(1024)(128)(2,1)S(1)}, bf16[1024]{0:T(1024)(128)(2,1)S(1)}) all-reduce(bf16[1024]{0:T(1024)(128)(2,1)S(1)} %dynamic-update-slice.6, bf16[1024]{0:T(1024)(128)(2,1)S(1)} %dynamic-update-slice.7), channel_id=1, replica_groups=mesh['shard'=8,'ctx'=2,'tp'=2] {'shard','ctx'}, use_global_device_ids=true, to_apply=%add | all-reduce | flops 2048 | bytes 8192 | tf_op jit(solution)/shard_map/while
  800.7 14.0 all-gather.10.cloned.1.call-done
  817.6 53.8 %all-gather.18.cloned.1.call-done = bf16[1024,512]{1,0:T(8,128)(2,1)} async-done(((bf16[64,512]{1,0:T(8,128)(2,1)}), bf16[1024,512]{1,0:T(8,128)(2,1)}) %all-gather.18.cloned.1.call-update) | async-done | bytes 1048592 | tf_op jit(solution)/shard_map/while/body/eval_jaxpr/all_gather | solution.py:352
  876.2 52.0 %all-gather.14.cloned.1.call-done = bf16[1024,512]{1,0:T(8,128)(2,1)} async-done(((bf16[64,512]{1,0:T(8,128)(2,1)}), bf16[1024,512]{1,0:T(8,128)(2,1)}) %all-gather.14.cloned.1.call-update) | async-done | bytes 1048592 | tf_op jit(solution)/shard_map/while/body/eval_jaxpr/all_gather | solution.py:350
  931.0 18.7 all-gather.12.cloned.1.call-done
  951.2 8.7 fusion.253
  982.0 48.6 %all-gather.16.cloned.1.call-done = bf16[1024,512]{1,0:T(8,128)(2,1)} async-done(((bf16[64,512]{1,0:T(8,128)(2,1)}), bf16[1024,512]{1,0:T(8,128)(2,1)}) %all-gather.16.cloned.1.call-update) | async-done | bytes 1048592 | tf_op jit(solution)/shard_map/while/body/eval_jaxpr/all_gather | solution.py:353
  1036.9 17.2 all-reduce.17.cloned.1.call-done
  1057.6 66.8 %all-gather.24.cloned.1.call-done = bf16[1024,1408]{1,0:T(8,128)(2,1)} async-done(((bf16[64,1408]{1,0:T(8,128)(2,1)}), bf16[1024,1408]{1,0:T(8,128)(2,1)}) %all-gather.24.cloned.1.call-update) | async-done | bytes 2883600 | tf_op jit(solution)/shard_map/while/body/eval_jaxpr/all_gather | solution.py:368
  1129.9 62.6 %all-gather.22.cloned.1.call-done = bf16[1024,1408]{1,0:T(8,128)(2,1)} async-done(((bf16[64,1408]{1,0:T(8,128)(2,1)}), bf16[1024,1408]{1,0:T(8,128)(2,1)}) %all-gather.22.cloned.1.call-update) | async-done | bytes 2883600 | tf_op jit(solution)/shard_map/while/body/eval_jaxpr/all_gather | solution.py:354
  1198.0 62.4 %all-gather.26.cloned.1.call-done = bf16[1024,1408]{1,0:T(8,128)(2,1)} async-done(((bf16[64,1408]{1,0:T(8,128)(2,1)}), bf16[1024,1408]{1,0:T(8,128)(2,1)}) %all-gather.26.cloned.1.call-update) | async-done | bytes 2883600 | tf_op jit(solution)/shard_map/while/body/eval_jaxpr/all_gather | solution.py:355
  1260.5 8.5 multiply_convert_fusion.8
  1275.3 20.1 all-reduce.19.cloned.1.call-done
  1301.1 14.7 multiply_reduce_fusion.9
  1329.5 8.6 fusion.263
  1366.3 30.4 %reduce-scatter.26.cloned.1.call-done = f32[512,512]{0,1:T(8,128)} async-done(((f32[1024,512]{0,1:T(8,128)}), f32[512,512]{0,1:T(8,128)}) %reduce-scatter.26.cloned.1.call-update) | async-done | bytes 1048592 | tf_op jit(solution)/shard_map/while/body/eval_jaxpr/reduce_scatter | solution.py:310
  1409.6 7.9 select_add_fusion.24
  1417.5 12.1 copy.47
  1430.2 17.0 while.58
  1478.0 76.2 %all-reduce.8 = (f32[1024]{0:T(1024)S(1)}, f32[1024]{0:T(1024)S(1)}, f32[32,8]{0,1:T(8,128)}) all-reduce(f32[1024]{0:T(1024)S(1)} %copy-done.44, f32[1024]{0:T(1024)S(1)} %copy-done.41, f32[32,8]{0,1:T(8,128)S(1)} %copy-done.38), channel_id=11, replica_groups=mesh['shard'=8,'ctx'=2,'tp'=2] {'shard','ctx'}, use_global_device_ids=true, to_apply=%region_28.29.clone | all-reduce | flops 2304 | bytes 18432
  1556.6 80.5 %reduce-scatter.12.cloned.1.call-done = f32[64,512]{1,0:T(8,128)} async-done(((f32[1024,512]{1,0:T(8,128)}), f32[64,512]{1,0:T(8,128)}) %reduce-scatter.12.cloned.1.call-update) | async-done | bytes 131088 | tf_op jit(solution)/shard_map/reduce_scatter | solution.py:391
  1637.1 80.6 %reduce-scatter.14.cloned.1.call-done = f32[64,512]{1,0:T(8,128)} async-done(((f32[1024,512]{1,0:T(8,128)}), f32[64,512]{1,0:T(8,128)}) %reduce-scatter.14.cloned.1.call-update) | async-done | bytes 131088 | tf_op jit(solution)/shard_map/reduce_scatter | solution.py:392
  1717.7 80.6 %reduce-scatter.16.cloned.1.call-done = f32[64,512]{1,0:T(8,128)} async-done(((f32[1024,512]{1,0:T(8,128)}), f32[64,512]{1,0:T(8,128)}) %reduce-scatter.16.cloned.1.call-update) | async-done | bytes 131088 | tf_op jit(solution)/shard_map/reduce_scatter | solution.py:393
  1798.3 126.4 %reduce-scatter.18.cloned.1.call-done = f32[64,1408]{1,0:T(8,128)} async-done(((f32[1024,1408]{1,0:T(8,128)}), f32[64,1408]{1,0:T(8,128)}) %reduce-scatter.18.cloned.1.call-update) | async-done | bytes 360464 | tf_op jit(solution)/shard_map/reduce_scatter | solution.py:394
  1924.7 129.8 %reduce-scatter.20.cloned.1.call-done = f32[64,1408]{1,0:T(8,128)} async-done(((f32[1024,1408]{1,0:T(8,128)}), f32[64,1408]{1,0:T(8,128)}) %reduce-scatter.20.cloned.1.call-update) | async-done | bytes 360464 | tf_op jit(solution)/shard_map/reduce_scatter | solution.py:395
  2054.5 129.7 %reduce-scatter.22.cloned.1.call-done = f32[64,1408]{1,0:T(8,128)} async-done(((f32[1024,1408]{1,0:T(8,128)}), f32[64,1408]{1,0:T(8,128)}) %reduce-scatter.22.cloned.1.call-update) | async-done | bytes 360464 | tf_op jit(solution)/shard_map/reduce_scatter | solution.py:396
  (447 shorter events, 346.8 us)
Async XLA Ops:
  25.2 17.9 copy-start.48
  25.2 17.9 copy-start.50
  25.2 17.9 copy-start.52
  25.2 17.9 copy-start.54
  43.3 61.7 %all-gather.10.cloned.1.call-start = ((), (), s32[]{:S(2)}) async-start(), calls=%async_computation.16 | async-start | bytes 1114112 | tf_op jit(solution)/shard_map/while/body/eval_jaxpr/all_gather | solution.py:351
  44.1 117.8 %all-gather.18.cloned.1.call-start = ((), (), s32[]{:S(2)}) async-start(), calls=%async_computation.20 | async-start | bytes 1114112 | tf_op jit(solution)/shard_map/while/body/eval_jaxpr/all_gather | solution.py:352
  44.8 174.0 %all-gather.14.cloned.1.call-start = ((), (), s32[]{:S(2)}) async-start(), calls=%async_computation.18 | async-start | bytes 1114112 | tf_op jit(solution)/shard_map/while/body/eval_jaxpr/all_gather | solution.py:350
  45.6 194.8 %all-gather.12.cloned.1.call-start = ((), (), s32[]{:S(2)}) async-start(), calls=%async_computation.17 | async-start | bytes 1572864 | tf_op jit(solution)/shard_map/while/body/eval_jaxpr/all_gather | solution.py:184
  90.8 128.0 %copy-start.31 = (f32[1024]{0:T(1024)}, f32[1024]{0:T(1024)S(1)}, u32[]{:S(2)}) copy-start(f32[1024]{0:T(1024)S(1)} %convert_element_type.309) | copy-start | bytes 12292 | tf_op jit(solution)/shard_map/while
  91.1 127.7 %copy-start.34 = (f32[512]{0:T(512)}, f32[512]{0:T(512)S(1)}, u32[]{:S(2)}) copy-start(f32[512]{0:T(512)S(1)} %add_rsqrt_fusion.4) | copy-start | bytes 6148 | tf_op jit(solution)/shard_map/while
  107.9 155.2 %all-gather.20.cloned.1.call-start = ((), (), s32[]{:S(2)}) async-start(), calls=%async_computation.21 | async-start | bytes 1572864 | tf_op jit(solution)/shard_map/while/body/eval_jaxpr/all_gather | solution.py:185
  164.8 156.3 %all-gather.16.cloned.1.call-start = ((), (), s32[]{:S(2)}) async-start(), calls=%async_computation.19 | async-start | bytes 1114112 | tf_op jit(solution)/shard_map/while/body/eval_jaxpr/all_gather | solution.py:353
  165.3 179.3 %all-reduce.17.cloned.1.call-start = ((), (), s32[]{:S(2)}) async-start(), calls=%async_computation.22 | async-start | bytes 4194304 | tf_op jit(solution)/shard_map/while/body/eval_jaxpr/psum | solution.py:204
  272.5 52.0 %copy-start.24 = (bf16[8,64,512]{2,1,0:T(8,128)(2,1)}, bf16[8,64,512]{2,1,0:T(8,128)(2,1)S(1)}, u32[]{:S(2)}) copy-start(bf16[8,64,512]{2,1,0:T(8,128)(2,1)S(1)} %fusion.255) | copy-start | bytes 1572868 | tf_op jit(solution)/shard_map/while
  324.4 90.4 %all-gather.24.cloned.1.call-start = ((), (), s32[]{:S(2)}) async-start(), calls=%async_computation.24 | async-start | bytes 3063808 | tf_op jit(solution)/shard_map/while/body/eval_jaxpr/all_gather | solution.py:368
  325.2 157.8 %all-gather.22.cloned.1.call-start = ((), (), s32[]{:S(2)}) async-start(), calls=%async_computation.23 | async-start | bytes 3063808 | tf_op jit(solution)/shard_map/while/body/eval_jaxpr/all_gather | solution.py:354
  325.9 225.0 %all-gather.26.cloned.1.call-start = ((), (), s32[]{:S(2)}) async-start(), calls=%async_computation.25 | async-start | bytes 3063808 | tf_op jit(solution)/shard_map/while/body/eval_jaxpr/all_gather | solution.py:355
  326.5 259.4 %all-reduce.19.cloned.1.call-start = ((), (), s32[]{:S(2)}) async-start(), calls=%async_computation.26 | async-start | bytes 4194304 | tf_op jit(solution)/shard_map/while/body/eval_jaxpr/psum | solution.py:268
  565.5 87.6 %reduce-scatter.24.cloned.1.call-start = ((), (), s32[]{:S(2)}) async-start(), calls=%async_computation.27 | async-start | bytes 3145728 | tf_op jit(solution)/shard_map/while/body/eval_jaxpr/reduce_scatter | solution.py:304
  619.9 67.4 %reduce-scatter.26.cloned.1.call-start = ((), (), s32[]{:S(2)}) async-start(), calls=%async_computation.28 | async-start | bytes 3145728 | tf_op jit(solution)/shard_map/while/body/eval_jaxpr/reduce_scatter | solution.py:310
  628.6 118.0 %all-reduce.21.cloned.1.call-start = ((), (), s32[]{:S(2)}) async-start(), calls=%async_computation.29 | async-start | bytes 8388608 | tf_op jit(solution)/shard_map/while/body/eval_jaxpr/psum | solution.py:323
  715.4 18.0 copy-start.36
  715.4 18.0 copy-start.32
  715.4 18.0 copy-start.35
  755.7 59.0 %all-gather.10.cloned.1.call-start = ((), (), s32[]{:S(2)}) async-start(), calls=%async_computation.16 | async-start | bytes 1114112 | tf_op jit(solution)/shard_map/while/body/eval_jaxpr/all_gather | solution.py:351
  756.3 115.1 %all-gather.18.cloned.1.call-start = ((), (), s32[]{:S(2)}) async-start(), calls=%async_computation.20 | async-start | bytes 1114112 | tf_op jit(solution)/shard_map/while/body/eval_jaxpr/all_gather | solution.py:352
  756.9 171.3 %all-gather.14.cloned.1.call-start = ((), (), s32[]{:S(2)}) async-start(), calls=%async_computation.18 | async-start | bytes 1114112 | tf_op jit(solution)/shard_map/while/body/eval_jaxpr/all_gather | solution.py:350
  757.5 192.2 %all-gather.12.cloned.1.call-start = ((), (), s32[]{:S(2)}) async-start(), calls=%async_computation.17 | async-start | bytes 1572864 | tf_op jit(solution)/shard_map/while/body/eval_jaxpr/all_gather | solution.py:184
  800.4 127.8 %copy-start.31 = (f32[1024]{0:T(1024)}, f32[1024]{0:T(1024)S(1)}, u32[]{:S(2)}) copy-start(f32[1024]{0:T(1024)S(1)} %convert_element_type.309) | copy-start | bytes 12292 | tf_op jit(solution)/shard_map/while
  800.7 127.5 %copy-start.34 = (f32[512]{0:T(512)}, f32[512]{0:T(512)S(1)}, u32[]{:S(2)}) copy-start(f32[512]{0:T(512)S(1)} %add_rsqrt_fusion.4) | copy-start | bytes 6148 | tf_op jit(solution)/shard_map/while
  817.6 155.0 %all-gather.20.cloned.1.call-start = ((), (), s32[]{:S(2)}) async-start(), calls=%async_computation.21 | async-start | bytes 1572864 | tf_op jit(solution)/shard_map/while/body/eval_jaxpr/all_gather | solution.py:185
  874.3 156.3 %all-gather.16.cloned.1.call-start = ((), (), s32[]{:S(2)}) async-start(), calls=%async_computation.19 | async-start | bytes 1114112 | tf_op jit(solution)/shard_map/while/body/eval_jaxpr/all_gather | solution.py:353
  874.9 179.3 %all-reduce.17.cloned.1.call-start = ((), (), s32[]{:S(2)}) async-start(), calls=%async_computation.22 | async-start | bytes 4194304 | tf_op jit(solution)/shard_map/while/body/eval_jaxpr/psum | solution.py:204
  982.0 52.0 %copy-start.24 = (bf16[8,64,512]{2,1,0:T(8,128)(2,1)}, bf16[8,64,512]{2,1,0:T(8,128)(2,1)S(1)}, u32[]{:S(2)}) copy-start(bf16[8,64,512]{2,1,0:T(8,128)(2,1)S(1)} %fusion.255) | copy-start | bytes 1572868 | tf_op jit(solution)/shard_map/while
  1034.0 90.4 %all-gather.24.cloned.1.call-start = ((), (), s32[]{:S(2)}) async-start(), calls=%async_computation.24 | async-start | bytes 3063808 | tf_op jit(solution)/shard_map/while/body/eval_jaxpr/all_gather | solution.py:368
  1034.7 157.8 %all-gather.22.cloned.1.call-start = ((), (), s32[]{:S(2)}) async-start(), calls=%async_computation.23 | async-start | bytes 3063808 | tf_op jit(solution)/shard_map/while/body/eval_jaxpr/all_gather | solution.py:354
  1035.5 225.0 %all-gather.26.cloned.1.call-start = ((), (), s32[]{:S(2)}) async-start(), calls=%async_computation.25 | async-start | bytes 3063808 | tf_op jit(solution)/shard_map/while/body/eval_jaxpr/all_gather | solution.py:355
  1036.0 259.4 %all-reduce.19.cloned.1.call-start = ((), (), s32[]{:S(2)}) async-start(), calls=%async_computation.26 | async-start | bytes 4194304 | tf_op jit(solution)/shard_map/while/body/eval_jaxpr/psum | solution.py:268
  1275.0 87.6 %reduce-scatter.24.cloned.1.call-start = ((), (), s32[]{:S(2)}) async-start(), calls=%async_computation.27 | async-start | bytes 3145728 | tf_op jit(solution)/shard_map/while/body/eval_jaxpr/reduce_scatter | solution.py:304
  1329.5 67.2 %reduce-scatter.26.cloned.1.call-start = ((), (), s32[]{:S(2)}) async-start(), calls=%async_computation.28 | async-start | bytes 3145728 | tf_op jit(solution)/shard_map/while/body/eval_jaxpr/reduce_scatter | solution.py:310
  1338.2 123.7 %all-reduce.21.cloned.1.call-start = ((), (), s32[]{:S(2)}) async-start(), calls=%async_computation.29 | async-start | bytes 8388608 | tf_op jit(solution)/shard_map/while/body/eval_jaxpr/psum | solution.py:323
  1472.2 84.5 %reduce-scatter.10.cloned.1.call-start = ((), (), s32[]{:S(2)}) async-start(), calls=%async_computation.9 | async-start | bytes 2228224 | tf_op jit(solution)/shard_map/reduce_scatter | solution.py:390
  1472.8 164.4 %reduce-scatter.12.cloned.1.call-start = ((), (), s32[]{:S(2)}) async-start(), calls=%async_computation.10 | async-start | bytes 2228224 | tf_op jit(solution)/shard_map/reduce_scatter | solution.py:391
  1473.3 244.4 %reduce-scatter.14.cloned.1.call-start = ((), (), s32[]{:S(2)}) async-start(), calls=%async_computation.11 | async-start | bytes 2228224 | tf_op jit(solution)/shard_map/reduce_scatter | solution.py:392
  1473.9 324.4 %reduce-scatter.16.cloned.1.call-start = ((), (), s32[]{:S(2)}) async-start(), calls=%async_computation.12 | async-start | bytes 2228224 | tf_op jit(solution)/shard_map/reduce_scatter | solution.py:393
  1474.7 450.0 %reduce-scatter.18.cloned.1.call-start = ((), (), s32[]{:S(2)}) async-start(), calls=%async_computation.13 | async-start | bytes 6127616 | tf_op jit(solution)/shard_map/reduce_scatter | solution.py:394
  1475.4 579.1 %reduce-scatter.20.cloned.1.call-start = ((), (), s32[]{:S(2)}) async-start(), calls=%async_computation.14 | async-start | bytes 6127616 | tf_op jit(solution)/shard_map/reduce_scatter | solution.py:395
  1476.2 708.0 %reduce-scatter.22.cloned.1.call-start = ((), (), s32[]{:S(2)}) async-start(), calls=%async_computation.15 | async-start | bytes 6127616 | tf_op jit(solution)/shard_map/reduce_scatter | solution.py:396
  (103 other events, 568.3 us)
Sparse Core Ops, SparseCore 0:
  46.9 58.0 all-gather.9
  107.8 54.0 all-gather.17
  164.7 54.0 all-gather.13
  220.2 20.0 all-gather.11
  241.7 21.2 all-gather.19
  265.7 55.3 all-gather.15
  324.6 20.0 all-reduce.16
  347.7 67.0 all-gather.23
  418.0 64.9 all-gather.21
  485.9 64.9 all-gather.25
  565.6 20.2 all-reduce.18
  620.1 32.9 reduce-scatter.23
  655.4 31.8 reduce-scatter.25
  692.4 28.5 all-reduce.20
  759.0 55.6 all-gather.9
  817.4 54.0 all-gather.17
  874.1 54.0 all-gather.13
  929.6 20.0 all-gather.11
  951.3 21.2 all-gather.19
  975.2 55.3 all-gather.15
  1034.1 20.0 all-reduce.16
  1057.3 67.0 all-gather.23
  1127.5 64.9 all-gather.21
  1195.5 64.9 all-gather.25
  1275.1 20.2 all-reduce.18
  1329.6 32.9 reduce-scatter.23
  1364.8 31.8 reduce-scatter.25
  1401.8 28.5 all-reduce.20
Sparse Core Ops, SparseCore 1:
  1475.5 81.1 reduce-scatter.9
  1559.3 77.7 reduce-scatter.11
  1639.9 77.8 reduce-scatter.13
  1720.6 77.6 reduce-scatter.15
  1801.2 123.4 reduce-scatter.17
  1927.6 126.8 reduce-scatter.19
  2057.2 126.8 reduce-scatter.21
where the time goes:
time: 2200 us; the launch traced here: 2190 us
  waiting for transfers between devices  1560 us (71%)
  matrix products  303 us (14%)
  blocking collectives  161 us (7%)
  local copies, waits for them, and re-layouts  90.7 us (4%)
  other arithmetic  55.2 us (3%)
    all_gather x2, waiting for transfers between devices, micro_step(): lax.all_gather(down_weight, ('shard', 'ctx'), axis=0, tiled=True)  134 us
    reduce_scatter x1, waiting for transfers between devices, shards(): lax.psum_scatter(grad_sums[5], ('shard', 'ctx'), scatter_dimension=0, til...  130 us
    reduce_scatter x1, waiting for transfers between devices, shards(): lax.psum_scatter(grad_sums[6], ('shard', 'ctx'), scatter_dimension=0, til...  130 us
    reduce_scatter x1, waiting for transfers between devices, shards(): lax.psum_scatter(grad_sums[4], ('shard', 'ctx'), scatter_dimension=0, til...  126 us
    all_gather x2, waiting for transfers between devices, micro_step(): lax.all_gather(gate_weight, ('shard', 'ctx'), axis=0, tiled=True)  125 us
    all_gather x2, waiting for transfers between devices, micro_step(): lax.all_gather(up_weight, ('shard', 'ctx'), axis=0, tiled=True)  125 us
    all_gather x2, waiting for transfers between devices, micro_step(): lax.all_gather(value_weight, ('shard', 'ctx'), axis=0, tiled=True)  108 us
    all_gather x2, waiting for transfers between devices, micro_step(): lax.all_gather(query_weight, ('shard', 'ctx'), axis=0, tiled=True)  104 us
  transfers between devices with their start and end apart: 35, of which 33 were waited for; matrix products, arithmetic and copies ran while one was open for 12% of the time, Pallas kernels for 0%

commit v1 on v0

v1 whole, which is shorter than its diff:
```python
import functools

import jax
import jax.numpy as jnp
from jax import lax
from jax.experimental import pallas as pl
from jax.experimental.pallas import tpu as pltpu
from jax.sharding import PartitionSpec as P

EPSILON = 1e-06
GELU_ROOT = 0.7978845608028654
GELU_CUBIC = 0.044715
MESH = pl.DeviceIdType.MESH
MIB = 1024 * 1024


BAND = 3
BLOCK = 128


def lane_head(rows, width, which):
    lanes = lax.broadcasted_iota(jnp.int32, (rows, width), 1)
    half = width // 2
    return (lanes < half) if which == 0 else (lanes >= half)


def bias_kernel(band_ref, bandt_ref, table_ref, bias_ref, biast_ref):
    rows = table_ref[0]
    for part in range(band_ref.shape[1] // 8):
        piece = band_ref[0, pl.ds(8 * part, 8), :]
        for col in range(BAND):
            index = piece[:, col * BLOCK : (col + 1) * BLOCK]
            got = jnp.take_along_axis(rows, index, axis=1)
            bias_ref[0, 0, pl.ds(8 * part, 8), col * BLOCK : (col + 1) * BLOCK] = got
    for part in range(bandt_ref.shape[1] // 8):
        index = bandt_ref[0, pl.ds(8 * part, 8), :]
        biast_ref[0, 0, pl.ds(8 * part, 8), :] = jnp.take_along_axis(rows, index, axis=1)


def bias_bands(band, bandt, table_rows):
    blocks = band.shape[0]
    heads = table_rows.shape[0]
    return pl.pallas_call(
        bias_kernel,
        grid=(blocks, heads),
        in_specs=[
            pl.BlockSpec((1, BLOCK, BAND * BLOCK), lambda i, h: (i, 0, 0)),
            pl.BlockSpec((1, BAND * BLOCK, BLOCK), lambda i, h: (i, 0, 0)),
            pl.BlockSpec((1, 8, 128), lambda i, h: (h, 0, 0)),
        ],
        out_specs=[
            pl.BlockSpec((1, 1, BLOCK, BAND * BLOCK), lambda i, h: (h, i, 0, 0)),
            pl.BlockSpec((1, 1, BAND * BLOCK, BLOCK), lambda i, h: (h, i, 0, 0)),
        ],
        out_shape=[
            jax.ShapeDtypeStruct((heads, blocks, BLOCK, BAND * BLOCK), jnp.float32),
            jax.ShapeDtypeStruct((heads, blocks, BAND * BLOCK, BLOCK), jnp.float32),
        ],
        name="bias_bands",
    )(band, bandt, table_rows)


def band_start(row_block, blocks):
    return jnp.clip(row_block - 1, 0, blocks - BAND)


def forward_kernel(q_ref, k_ref, v_ref, kaux_ref, qaux_ref, bias_ref, out_ref, lse_ref, s_ref, *, blocks):
    step = pl.program_id(1)
    rows = q_ref.shape[0]
    subs = rows // BLOCK
    pair = q_ref[...]
    keys = jnp.concatenate([k_ref[...], kaux_ref[...]], axis=1)
    outs = []
    for head in range(2):
        aux = jnp.concatenate(
            [jnp.broadcast_to(qaux_ref[head, sub : sub + 1, :], (BLOCK, 128)) for sub in range(subs)], axis=0
        ).astype(jnp.bfloat16)
        masked = jnp.where(lane_head(rows, 128, head), pair, jnp.zeros_like(pair))
        left = jnp.concatenate([masked, aux], axis=1)
        s_ref[...] = lax.dot_general(
            left, keys, (((1,), (1,)), ((), ())), preferred_element_type=jnp.float32
        )
        for sub in range(subs):
            start = pl.multiple_of(band_start(step * subs + sub, blocks) * BLOCK, BLOCK)
            s_ref[sub * BLOCK : (sub + 1) * BLOCK, pl.ds(start, BAND * BLOCK)] += bias_ref[head, sub]
        scores = s_ref[...]
        highest = jnp.max(scores, axis=1, keepdims=True)
        exponent = jnp.exp(scores - highest)
        total = jnp.sum(exponent, axis=1, keepdims=True)
        outs.append(
            jnp.dot(exponent.astype(jnp.bfloat16), v_ref[...], preferred_element_type=jnp.float32)
            * (1.0 / total)
        )
        lse = jnp.broadcast_to(highest + jnp.log(total), (rows, 128))
        lse_ref[0, head : head + 1, :] = jnp.transpose(lse)[0:1, :]
    out_ref[...] = jnp.where(lane_head(rows, 128, 0), outs[0], outs[1]).astype(jnp.bfloat16)


def attention_forward(qkv, kaux, qaux, bias):
    length = qkv.shape[0]
    heads, blocks = bias.shape[:2]
    pairs = heads // 2
    rows = 256
    subs = rows // BLOCK
    return pl.pallas_call(
        functools.partial(forward_kernel, blocks=blocks),
        grid=(pairs, length // rows),
        in_specs=[
            pl.BlockSpec((rows, 128), lambda p, i: (i, p)),
            pl.BlockSpec((length, 128), lambda p, i: (0, pairs + p)),
            pl.BlockSpec((length, 128), lambda p, i: (0, 2 * pairs + p)),
            pl.BlockSpec((length, 128), lambda p, i: (0, 0)),
            pl.BlockSpec((2, None, subs, 128), lambda p, i: (p, i, 0, 0)),
            pl.BlockSpec((2, subs, BLOCK, BAND * BLOCK), lambda p, i: (p, i, 0, 0)),
        ],
        out_specs=[
            pl.BlockSpec((rows, 128), lambda p, i: (i, p)),
            pl.BlockSpec((1, 2, rows), lambda p, i: (p, 0, i)),
        ],
        out_shape=[
            jax.ShapeDtypeStruct((length, pairs * 128), jnp.bfloat16),
            jax.ShapeDtypeStruct((pairs, 2, length), jnp.float32),
        ],
        scratch_shapes=[pltpu.VMEM((rows, length), jnp.float32)],
        compiler_params=pltpu.CompilerParams(vmem_limit_bytes=40 * 1024 * 1024),
        name="attention_forward",
    )(qkv, qkv, qkv, kaux, qaux.reshape(heads, blocks // subs, subs, 128), bias)


def backward_kernel(
    q_ref, k_ref, v_ref, kaux_ref, qaux_ref, bias_ref, lse_ref, do_ref,
    dq_ref, dk_ref, dv_ref, gs_ref, sums_ref, s_ref, g_ref, dk_acc, dv_acc, *, blocks
):
    step = pl.program_id(1)
    steps = pl.num_programs(1)
    rows = q_ref.shape[0]
    subs = rows // BLOCK

    @pl.when(step == 0)
    def _():
        dk_acc[...] = jnp.zeros_like(dk_acc)
        dv_acc[...] = jnp.zeros_like(dv_acc)

    pair = q_ref[...]
    grad = do_ref[...]
    key_pair = k_ref[...]
    keys = jnp.concatenate([key_pair, kaux_ref[...]], axis=1)
    last = (((1,), (1,)), ((), ()))
    dq = None
    for head in range(2):
        here = lane_head(rows, 128, head)
        aux = jnp.concatenate(
            [jnp.broadcast_to(qaux_ref[head, sub : sub + 1, :], (BLOCK, 128)) for sub in range(subs)], axis=0
        ).astype(jnp.bfloat16)
        q_masked = jnp.where(here, pair, jnp.zeros_like(pair))
        do_masked = jnp.where(here, grad, jnp.zeros_like(grad))
        s_ref[...] = lax.dot_general(
            keys, jnp.concatenate([q_masked, aux], axis=1), last, preferred_element_type=jnp.float32
        )
        for sub in range(subs):
            start = pl.multiple_of(band_start(step * subs + sub, blocks) * BLOCK, BLOCK)
            s_ref[pl.ds(start, BAND * BLOCK), sub * BLOCK : (sub + 1) * BLOCK] += bias_ref[head, sub]
        soft = jnp.exp(s_ref[...] - lse_ref[0, head : head + 1, :])
        dv_acc[...] += jnp.dot(soft.astype(jnp.bfloat16), do_masked, preferred_element_type=jnp.float32)
        grad_probs = lax.dot_general(v_ref[...], do_masked, last, preferred_element_type=jnp.float32)
        weighted = jnp.sum(soft * grad_probs, axis=0, keepdims=True)
        grad_scores = (soft * (grad_probs - weighted)).astype(jnp.bfloat16)
        g_ref[...] = grad_scores
        dk_acc[...] += jnp.dot(grad_scores, q_masked, preferred_element_type=jnp.float32)
        k_masked = jnp.where(lane_head(key_pair.shape[0], 128, head), key_pair, jnp.zeros_like(key_pair))
        part = lax.dot_general(
            grad_scores, k_masked, (((0,), (0,)), ((), ())), preferred_element_type=jnp.float32
        )
        dq = part if dq is None else dq + part
        for sub in range(subs):
            start = pl.multiple_of(band_start(step * subs + sub, blocks) * BLOCK, BLOCK)
            gs_ref[head, sub] = g_ref[pl.ds(start, BAND * BLOCK), sub * BLOCK : (sub + 1) * BLOCK]
        for block in range(blocks):
            sums_ref[head, block : block + 1, :] = jnp.sum(
                grad_scores[block * BLOCK : (block + 1) * BLOCK, :].astype(jnp.float32), axis=0, keepdims=True
            )
    dq_ref[...] = dq.astype(jnp.bfloat16)

    @pl.when(step == steps - 1)
    def _():
        dk_ref[...] = dk_acc[...].astype(jnp.bfloat16)
        dv_ref[...] = dv_acc[...].astype(jnp.bfloat16)


def attention_backward(qkv, kaux, qaux, biast, lse, grad_attended):
    length = qkv.shape[0]
    heads, blocks = biast.shape[:2]
    pairs = heads // 2
    rows = 256
    subs = rows // BLOCK
    wide = jax.ShapeDtypeStruct((length, pairs * 128), jnp.bfloat16)
    return pl.pallas_call(
        functools.partial(backward_kernel, blocks=blocks),
        grid=(pairs, length // rows),
        in_specs=[
            pl.BlockSpec((rows, 128), lambda p, i: (i, p)),
            pl.BlockSpec((length, 128), lambda p, i: (0, pairs + p)),
            pl.BlockSpec((length, 128), lambda p, i: (0, 2 * pairs + p)),
            pl.BlockSpec((length, 128), lambda p, i: (0, 0)),
            pl.BlockSpec((2, None, subs, 128), lambda p, i: (p, i, 0, 0)),
            pl.BlockSpec((2, subs, BAND * BLOCK, BLOCK), lambda p, i: (p, i, 0, 0)),
            pl.BlockSpec((1, 2, rows), lambda p, i: (p, 0, i)),
            pl.BlockSpec((rows, 128), lambda p, i: (i, p)),
        ],
        out_specs=[
            pl.BlockSpec((rows, 128), lambda p, i: (i, p)),
            pl.BlockSpec((length, 128), lambda p, i: (0, p)),
            pl.BlockSpec((length, 128), lambda p, i: (0, p)),
            pl.BlockSpec((2, subs, BAND * BLOCK, BLOCK), lambda p, i: (p, i, 0, 0)),
            pl.BlockSpec((2, blocks, rows), lambda p, i: (p, 0, i)),
        ],
        out_shape=[
            wide,
            wide,
            wide,
            jax.ShapeDtypeStruct((heads, blocks, BAND * BLOCK, BLOCK), jnp.bfloat16),
            jax.ShapeDtypeStruct((heads, blocks, length), jnp.float32),
        ],
        scratch_shapes=[
            pltpu.VMEM((length, rows), jnp.float32),
            pltpu.VMEM((length, rows), jnp.bfloat16),
            pltpu.VMEM((length, 128), jnp.float32),
            pltpu.VMEM((length, 128), jnp.float32),
        ],
        compiler_params=pltpu.CompilerParams(vmem_limit_bytes=40 * 1024 * 1024),
        name="attention_backward",
    )(qkv, qkv, qkv, kaux, qaux.reshape(heads, blocks // subs, subs, 128), biast, lse, grad_attended)


GROUP = 16


def table_kernel(bandt_ref, gs_ref, out_ref, acc_ref, *, buckets):
    step = pl.program_id(0)

    @pl.when(step == 0)
    def _():
        acc_ref[...] = jnp.zeros_like(acc_ref)

    heads = gs_ref.shape[0]

    def one(group, carry):
        start = pl.multiple_of(group * GROUP, GROUP)
        grads = jnp.concatenate(
            [gs_ref[:, two, pl.ds(start, GROUP), :].reshape(heads * GROUP, BLOCK) for two in range(2)], axis=1
        )
        index = jnp.concatenate([bandt_ref[two, pl.ds(start, GROUP), :] for two in range(2)], axis=1)
        index = index.astype(jnp.float32)
        hot = jnp.concatenate(
            [jnp.where(index == float(b), 1.0, 0.0) for b in range(buckets)], axis=0
        ).astype(jnp.bfloat16)
        acc_ref[...] += lax.dot_general(
            hot, grads, (((1,), (1,)), ((), ())), preferred_element_type=jnp.float32
        )
        return carry

    lax.fori_loop(0, BAND * BLOCK // GROUP, one, 0)

    @pl.when(step == pl.num_programs(0) - 1)
    def _():
        row = lax.broadcasted_iota(jnp.int32, acc_ref.shape, 0) % GROUP
        col = lax.broadcasted_iota(jnp.int32, acc_ref.shape, 1) % GROUP
        out_ref[...] = jnp.where(row == col, acc_ref[...], 0.0)


def table_band(bandt, gs, buckets):
    heads, blocks = gs.shape[:2]
    out = pl.pallas_call(
        functools.partial(table_kernel, buckets=buckets),
        grid=(blocks // 2,),
        in_specs=[
            pl.BlockSpec((2, BAND * BLOCK, BLOCK), lambda i: (i, 0, 0)),
            pl.BlockSpec((heads, 2, BAND * BLOCK, BLOCK), lambda i: (0, i, 0, 0)),
        ],
        out_specs=pl.BlockSpec((buckets * GROUP, heads * GROUP), lambda i: (0, 0)),
        out_shape=jax.ShapeDtypeStruct((buckets * GROUP, heads * GROUP), jnp.float32),
        scratch_shapes=[pltpu.VMEM((buckets * GROUP, heads * GROUP), jnp.float32)],
        compiler_params=pltpu.CompilerParams(vmem_limit_bytes=40 * 1024 * 1024),
        name="table_band",
    )(bandt, gs)
    return out.reshape(buckets, GROUP, heads, GROUP).sum((1, 3))
def split_columns(start, stop, pieces):
    tiles = (stop - start) // 128
    edges = [start + 128 * (tiles * i // pieces) for i in range(pieces + 1)]
    return [(a, b) for a, b in zip(edges, edges[1:]) if b > a]


class Place:
    def __init__(self, shard_size):
        self.deep = shard_size // 2
        shard = lax.axis_index("shard")
        self.z = shard // 2
        self.y = shard % 2
        self.x = lax.axis_index("ctx")
        self.c = lax.axis_index("tp")

    def device(self, z=None, y=None, x=None, c=None):
        z = self.z if z is None else z
        y = self.y if y is None else y
        x = self.x if x is None else x
        c = self.c if c is None else c
        return (z * 2 + y, x, c)

    def line(self, distance):
        return (self.z + distance) % self.deep

    def peers(self):
        others = [self.device(z=self.line(d)) for d in range(1, self.deep)]
        return others + [self.device(y=1 - self.y), self.device(x=1 - self.x), self.device(c=1 - self.c)]


def meet(place):
    barrier = pltpu.get_barrier_semaphore()
    peers = place.peers()
    for peer in peers:
        pl.semaphore_signal(barrier, inc=1, device_id=peer, device_id_type=MESH)
    pl.semaphore_wait(barrier, len(peers))


def send(source, target, send_sem, recv_sem, device):
    return pltpu.make_async_remote_copy(
        src_ref=source, dst_ref=target, send_sem=send_sem, recv_sem=recv_sem, device_id=device, device_id_type=MESH
    )


def gather_kernel(shard_size, chunks, own_ref, full_ref, local_sem, send_line, recv_line, send_near, recv_near, send_far, recv_far):
    place = Place(shard_size)
    z, y, x, deep = place.z, place.y, place.x, place.deep
    meet(place)

    def line_copy(j, d):
        a, b, _ = chunks[j]
        return send(
            own_ref.at[:, a:b],
            full_ref.at[z, y, x, :, a:b],
            send_line.at[j, d - 1],
            recv_line.at[j, d - 1],
            place.device(z=place.line(d)),
        )

    def near_copy(j):
        a, b, kind = chunks[j]
        here = full_ref.at[:, y, x, :, a:b]
        device = place.device(y=1 - y) if kind == 0 else place.device(x=1 - x)
        return send(here, here, send_near.at[j], recv_near.at[j], device)

    def far_copy(j):
        a, b, kind = chunks[j]
        here = full_ref.at[:, :, x, :, a:b] if kind == 0 else full_ref.at[:, y, :, :, a:b]
        device = place.device(x=1 - x) if kind == 0 else place.device(y=1 - y)
        return send(here, here, send_far.at[j], recv_far.at[j], device)

    count = len(chunks)
    own = pltpu.make_async_copy(own_ref, full_ref.at[z, y, x], local_sem)
    own.start()
    for j in range(count):
        for d in range(1, deep):
            line_copy(j, d).start()
    own.wait()
    for j in range(count + 1):
        if j < count:
            for d in range(1, deep):
                line_copy(j, d).wait_recv()
            near_copy(j).start()
        if j > 0:
            near_copy(j - 1).wait_recv()
            far_copy(j - 1).start()
    for j in range(count):
        far_copy(j).wait_recv()
    for j in range(count):
        for d in range(1, deep):
            line_copy(j, d).wait_send()
        near_copy(j).wait_send()
        far_copy(j).wait_send()


def gather_weights(shard_size, own, chunks):
    rows, width = own.shape
    deep = shard_size // 2
    count = len(chunks)
    return pl.pallas_call(
        functools.partial(gather_kernel, shard_size, chunks),
        out_shape=jax.ShapeDtypeStruct((deep, 2, 2, rows, width), own.dtype),
        in_specs=[pl.BlockSpec(memory_space=pl.ANY)],
        out_specs=pl.BlockSpec(memory_space=pl.ANY),
        scratch_shapes=[
            pltpu.SemaphoreType.DMA,
            pltpu.SemaphoreType.DMA((count, deep - 1)),
            pltpu.SemaphoreType.DMA((count, deep - 1)),
            pltpu.SemaphoreType.DMA((count,)),
            pltpu.SemaphoreType.DMA((count,)),
            pltpu.SemaphoreType.DMA((count,)),
            pltpu.SemaphoreType.DMA((count,)),
        ],
        compiler_params=pltpu.CompilerParams(collective_id=1, has_side_effects=True),
        name="gather_weights",
    )(own)


def scatter_kernel(shard_size, chunks, tensors, *refs):
    grad_refs, refs = refs[:tensors], refs[tensors:]
    small_ref, refs = refs[0], refs[1:]
    out_refs, refs = refs[:tensors], refs[tensors:]
    small_out, refs = refs[0], refs[1:]
    count = len(chunks)
    first_bufs, refs = refs[:count], refs[count:]
    own_bufs, refs = refs[:count], refs[count:]
    second_bufs, refs = refs[:count], refs[count:]
    line_bufs, refs = refs[:count], refs[count:]
    (
        small_x, small_y, small_z, small_c, hold_x, hold_y, hold_z,
        own_sem, send_first, recv_first, send_second, recv_second, send_line, recv_line,
        small_send, small_recv,
    ) = refs
    place = Place(shard_size)
    z, y, x, deep = place.z, place.y, place.x, place.deep
    meet(place)

    def first_copy(j):
        t, a, b, kind = chunks[j]
        grads = grad_refs[t]
        source = grads.at[:, :, 1 - x, :, a:b] if kind == 0 else grads.at[:, 1 - y, :, :, a:b]
        device = place.device(x=1 - x) if kind == 0 else place.device(y=1 - y)
        return send(source, first_bufs[j], send_first.at[j], recv_first.at[j], device)

    def own_copy(j):
        t, a, b, kind = chunks[j]
        grads = grad_refs[t]
        source = grads.at[:, :, x, :, a:b] if kind == 0 else grads.at[:, y, :, :, a:b]
        return pltpu.make_async_copy(source, own_bufs[j], own_sem.at[j])

    def second_copy(j):
        kind = chunks[j][3]
        mine = y if kind == 0 else x
        device = place.device(y=1 - y) if kind == 0 else place.device(x=1 - x)
        return send(own_bufs[j].at[:, 1 - mine], second_bufs[j], send_second.at[j], recv_second.at[j], device)

    def line_copy(j, d):
        kind = chunks[j][3]
        mine = y if kind == 0 else x
        return send(
            own_bufs[j].at[place.line(d), mine],
            line_bufs[j].at[d - 1],
            send_line.at[j, d - 1],
            recv_line.at[j, d - 1],
            place.device(z=place.line(d)),
        )

    def small_line(d):
        return send(hold_z.at[z], hold_z.at[z], small_send.at[d + 2], small_recv.at[d + 2], place.device(z=place.line(d)))

    for j in range(count):
        first_copy(j).start()
        own_copy(j).start()

    step = send(small_ref, small_x, small_send.at[0], small_recv.at[0], place.device(x=1 - x))
    step.start()
    step.wait()
    hold_x[...] = small_ref[...] + small_x[...]
    step = send(hold_x, small_y, small_send.at[1], small_recv.at[1], place.device(y=1 - y))
    step.start()
    step.wait()
    hold_z[z] = hold_x[...] + small_y[...]
    for d in range(1, deep):
        small_line(d).start()
    for d in range(1, deep):
        small_line(d).wait()
    hold_y[...] = jnp.sum(hold_z[...], axis=0)
    step = send(hold_y, small_c, small_send.at[2], small_recv.at[2], place.device(c=1 - place.c))
    step.start()
    step.wait()
    small_out[0] = hold_y[...]
    small_out[1] = hold_y[...] + small_c[...]

    def add_first(j):
        first_copy(j).wait_recv()
        own_copy(j).wait()

        def body(i, carry):
            for k in range(2):
                own_bufs[j][i, k] = (
                    own_bufs[j][i, k].astype(jnp.float32) + first_bufs[j][i, k].astype(jnp.float32)
                ).astype(jnp.bfloat16)
            return carry

        lax.fori_loop(0, deep, body, 0)
        second_copy(j).start()

    def add_second(j):
        second_copy(j).wait_recv()
        kind = chunks[j][3]
        mine = y if kind == 0 else x

        def body(i, carry):
            own_bufs[j][i, mine] = (
                own_bufs[j][i, mine].astype(jnp.float32) + second_bufs[j][i].astype(jnp.float32)
            ).astype(jnp.bfloat16)
            return carry

        lax.fori_loop(0, deep, body, 0)
        for d in range(1, deep):
            line_copy(j, d).start()

    def add_line(j):
        t, a, b, kind = chunks[j]
        mine = y if kind == 0 else x
        total = own_bufs[j][z, mine].astype(jnp.float32)
        for d in range(1, deep):
            line_copy(j, d).wait_recv()
            total = total + line_bufs[j][d - 1].astype(jnp.float32)
        out_refs[t][:, a:b] = total

    for j in range(count + 2):
        if j < count:
            add_first(j)
        if 0 < j <= count:
            add_second(j - 1)
        if j > 1:
            add_line(j - 2)
    for j in range(count):
        first_copy(j).wait_send()
        second_copy(j).wait_send()
        for d in range(1, deep):
            line_copy(j, d).wait_send()


def scatter_gradients(shard_size, grads, small, chunks):
    deep = shard_size // 2
    rows = grads[0].shape[3]
    tensors, count = len(grads), len(chunks)
    widths = [b - a for _, a, b, _ in chunks]
    low = jnp.bfloat16
    dma = pltpu.SemaphoreType.DMA
    small_buffer = pltpu.VMEM(small.shape, jnp.float32)
    vmem = pl.BlockSpec(memory_space=pltpu.VMEM)
    return pl.pallas_call(
        functools.partial(scatter_kernel, shard_size, chunks, tensors),
        out_shape=[jax.ShapeDtypeStruct((rows, g.shape[4]), jnp.float32) for g in grads]
        + [jax.ShapeDtypeStruct((2,) + small.shape, jnp.float32)],
        in_specs=[pl.BlockSpec(memory_space=pl.ANY)] * tensors + [vmem],
        out_specs=[vmem] * (tensors + 1),
        scratch_shapes=[pltpu.VMEM((deep, 2, rows, w), low) for w in widths]
        + [pltpu.VMEM((deep, 2, rows, w), low) for w in widths]
        + [pltpu.VMEM((deep, rows, w), low) for w in widths]
        + [pltpu.VMEM((deep - 1, rows, w), low) for w in widths]
        + [small_buffer, small_buffer, pltpu.VMEM((deep,) + small.shape, jnp.float32), small_buffer]
        + [small_buffer, small_buffer, pltpu.VMEM((deep,) + small.shape, jnp.float32)]
        + [dma((count,))] * 5
        + [dma((count, deep - 1))] * 2
        + [dma((deep + 2,))] * 2,
        compiler_params=pltpu.CompilerParams(
            collective_id=2, has_side_effects=True, vmem_limit_bytes=48 * MIB
        ),
        name="scatter_gradients",
    )(*grads, small)


def gelu_parts(gate):
    tangent = jnp.tanh(GELU_ROOT * (gate + GELU_CUBIC * gate * gate * gate))
    value = 0.5 * gate * (1.0 + tangent)
    slope = 0.5 * (1.0 + tangent) + 0.5 * gate * (1.0 - tangent * tangent) * GELU_ROOT * (
        1.0 + 3.0 * GELU_CUBIC * gate * gate
    )
    return value, slope


def normalize(tokens_in):
    inverse = lax.rsqrt(jnp.mean(tokens_in * tokens_in, axis=-1, keepdims=True) + EPSILON)
    return tokens_in * inverse, inverse


def normalize_back(grad, normal, inverse, gain):
    scaled = grad * gain
    back = inverse * (scaled - normal * jnp.mean(scaled * normal, axis=-1, keepdims=True))
    axes = tuple(range(grad.ndim - 1))
    return back, jnp.sum(grad * normal, axis=axes)


def dot(a, b, left, right, kind=jnp.float32):
    return lax.dot_general(a, b, (((left,), (right,)), ((), ())), preferred_element_type=jnp.float32).astype(kind)


def swap(values, axis):
    return lax.ppermute(values, axis, [(0, 1), (1, 0)])


def ordered(mine, other, place, axis):
    first = place == 0
    return jnp.stack([jnp.where(first, mine, other), jnp.where(first, other, mine)], axis=axis)


def take(values, index, axis):
    return lax.dynamic_index_in_dim(values, index, axis, keepdims=False)


def shards(
    inputs, cotangent, lengths, buckets,
    query_weight, key_weight, value_weight, projection_weight, gate_weight, up_weight, down_weight,
    attention_gain, feedforward_gain, bias_table,
):
    low = jnp.bfloat16
    x, c = lax.axis_index("ctx"), lax.axis_index("tp")
    shard_size = lax.axis_size("shard")
    half, width = inputs.shape[1:]
    quarter = half // 2
    length = 2 * half
    blocks = length // BLOCK
    bucket_count, heads = bias_table.shape
    inner = query_weight.shape[1]
    hidden_width = gate_weight.shape[1]

    gains = jnp.pad(jnp.stack([attention_gain, feedforward_gain], axis=1), ((0, 0), (0, 126)))
    own = jnp.concatenate(
        [query_weight, key_weight, value_weight, gains, projection_weight, gate_weight, up_weight, down_weight], axis=1
    )
    at_gain = 3 * inner
    at_project = at_gain + 128
    at_gate = at_project + inner
    at_up = at_gate + hidden_width
    at_down = at_up + hidden_width
    at_end = at_down + hidden_width
    pieces = split_columns(0, at_project, 2) + split_columns(at_project, at_gate, 1) + split_columns(at_gate, at_end, 6)
    chunks = [(a, b, i % 2) for i, (a, b) in enumerate(pieces)]
    full = gather_weights(shard_size, own, chunks).reshape(width, at_end)
    qkv_full = full[:, :at_gain]
    project_full = full[:, at_project:at_gate]
    gate_full = full[:, at_gate:at_up]
    up_full = full[:, at_up:at_down]
    down_full = full[:, at_down:at_end]
    gain_one = full[:, at_gain].astype(jnp.float32)
    gain_two = full[:, at_gain + 1].astype(jnp.float32)

    sequence_length = take(lengths[:, 0], x, 0)
    both = jnp.stack([inputs, cotangent])
    away = take(both, 1 - x, 1)
    arrived = swap(lax.dynamic_slice_in_dim(away, c * quarter, quarter, 1), "ctx")
    arrived = ordered(arrived, swap(arrived, "tp"), c, 1).reshape(2, half, width)
    whole = ordered(take(both, x, 1), arrived, x, 1)
    tokens, cots = whole[0].reshape(length, width), whole[1].reshape(length, width)

    starts = [min(max(i - 1, 0), blocks - BAND) * BLOCK for i in range(blocks)]
    start_of = jnp.asarray(starts, jnp.int32)
    own_band = jnp.stack(
        [
            lax.dynamic_slice(buckets, (i * BLOCK, start_of[x * (blocks // 2) + i]), (BLOCK, BAND * BLOCK))
            for i in range(blocks // 2)
        ]
    ).astype(low)
    band = ordered(own_band, swap(own_band, "ctx"), x, 0).reshape(blocks, BLOCK, BAND * BLOCK).astype(jnp.int32)
    bandt = jnp.swapaxes(band, 1, 2)
    table = bias_table.astype(jnp.float32)
    table_rows = jnp.broadcast_to(
        jnp.pad(table.T, ((0, 0), (0, 128 - bucket_count)))[:, None, :], (heads, 8, 128)
    )
    bias, biast = bias_bands(band, bandt, table_rows)
    block_at = jnp.arange(blocks) * BLOCK
    below = (block_at[None, :] < start_of[:, None])[None]
    above = (block_at[None, :] >= start_of[:, None] + BAND * BLOCK)[None]
    far_low, far_high = bucket_count // 2 - 1, bucket_count - 1
    constant = jnp.where(below, table[far_low][:, None, None], 0.0) + jnp.where(above, table[far_high][:, None, None], 0.0)
    qaux = jnp.concatenate(
        [constant, jnp.ones((heads, blocks, 1)), jnp.zeros((heads, blocks, 127 - blocks))], axis=-1
    )
    slots = jnp.arange(length, dtype=jnp.int32)
    kaux = jnp.concatenate(
        [
            (slots[:, None] // BLOCK == jnp.arange(blocks)[None, :]).astype(jnp.float32),
            jnp.where(slots < sequence_length, 0.0, -1e30)[:, None],
            jnp.zeros((length, 127 - blocks)),
        ],
        axis=1,
    ).astype(low)

    present = tokens.astype(jnp.float32)
    normal_one, inverse_one = normalize(present)
    normed_one = (normal_one * gain_one).astype(low)
    qkv = dot(normed_one, qkv_full, 1, 0, low)
    attended, lse = attention_forward(qkv, kaux, qaux, bias)
    grid = (2, 2, quarter, width)

    def reduce_rows(partial):
        parts = partial.reshape(grid)
        return take(parts, c, 1) + swap(take(parts, 1 - c, 1).astype(low), "tp").astype(jnp.float32)

    def share_rows(mine):
        return ordered(mine, swap(mine, "tp"), c, 1).reshape(length, width)

    def own_rows(values):
        return take(values.reshape(grid), c, 1)

    middle = own_rows(present) + reduce_rows(dot(attended, project_full, 1, 1))
    normal_two, inverse_two = normalize(middle)
    normed_two = share_rows((normal_two * gain_two).astype(low))
    gate = dot(normed_two, gate_full, 1, 0)
    up = dot(normed_two, up_full, 1, 0)
    value, slope = gelu_parts(gate)
    hidden = (value * up).astype(low)
    output = (middle + reduce_rows(dot(hidden, down_full, 1, 1))).astype(low)

    live = (slots < sequence_length).astype(jnp.float32)[:, None]
    grad_out = cots.astype(jnp.float32) * live
    grad_low = grad_out.astype(low)
    grad_down = dot(grad_low, hidden, 0, 0, low)
    grad_hidden = dot(grad_low, down_full, 1, 0)
    grad_gate = (grad_hidden * up * slope).astype(low)
    grad_up = (grad_hidden * value).astype(low)
    grad_gate_weight = dot(normed_two, grad_gate, 0, 0, low)
    grad_up_weight = dot(normed_two, grad_up, 0, 0, low)
    grad_two = reduce_rows(dot(grad_gate, gate_full, 1, 1) + dot(grad_up, up_full, 1, 1))
    back_two, gain_two_part = normalize_back(grad_two, normal_two, inverse_two, gain_two)
    grad_middle = own_rows(grad_out) + back_two
    grad_branch = share_rows(grad_middle.astype(low))
    grad_project = dot(grad_branch, attended, 0, 0, low)
    grad_attended = dot(grad_branch, project_full, 1, 0, low)
    grad_q, grad_k, grad_v, band_grads, sums = attention_backward(qkv, kaux, qaux, biast, lse, grad_attended)
    table_grad = table_band(bandt, band_grads, bucket_count)
    sums = sums.reshape(heads, blocks, blocks, BLOCK).sum(-1)
    table_grad = table_grad.at[far_low].add(jnp.sum(jnp.where(jnp.swapaxes(below, 1, 2), sums, 0.0), axis=(1, 2)))
    table_grad = table_grad.at[far_high].add(jnp.sum(jnp.where(jnp.swapaxes(above, 1, 2), sums, 0.0), axis=(1, 2)))
    grad_query = dot(normed_one, grad_q, 0, 0, low)
    grad_key = dot(normed_one, grad_k, 0, 0, low)
    grad_value = dot(normed_one, grad_v, 0, 0, low)
    grad_one = reduce_rows(
        dot(grad_q, qkv_full[:, :inner], 1, 1)
        + dot(grad_k, qkv_full[:, inner : 2 * inner], 1, 1)
        + dot(grad_v, qkv_full[:, 2 * inner :], 1, 1)
    )
    back_one, gain_one_part = normalize_back(grad_one, own_rows(normal_one), take(inverse_one.reshape(2, 2, quarter, 1), c, 1), gain_one)
    input_grad = (grad_middle + back_one).astype(low)

    def to_owners(mine):
        kept, leaving = take(mine, x, 0), take(mine, 1 - x, 0)
        pair = ordered(kept, swap(leaving, "ctx"), x, 0)
        return ordered(pair, swap(pair, "tp"), c, 1).reshape(2, half, width)

    output = to_owners(output)
    input_grad = to_owners(input_grad).astype(jnp.float32)

    rows = query_weight.shape[0]
    small = jnp.concatenate(
        [gain_one_part.reshape(-1, 128), gain_two_part.reshape(-1, 128), table_grad.reshape(-1, 128)], axis=0
    )
    used = small.shape[0]
    small = jnp.pad(small, ((0, -used % 8), (0, 0)))
    grads = [
        g.reshape(shard_size // 2, 2, 2, rows, g.shape[1])
        for g in (grad_down, grad_gate_weight, grad_up_weight, grad_project, grad_query, grad_key, grad_value)
    ]
    cuts = []
    for t, g in enumerate(grads):
        cuts += [(t, a, b) for a, b in split_columns(0, g.shape[4], 2 if t < 3 else 1)]
    cuts = [(t, a, b, i % 2) for i, (t, a, b) in enumerate(cuts)]
    *sums_out, small_out = scatter_gradients(shard_size, grads, small, cuts)
    down, gate_w, up_w, project, query, key, value_w = sums_out
    lines = width // 128
    me = lax.axis_index("shard") * 2 + x

    def own_gain(part):
        return lax.dynamic_slice_in_dim(small_out[1, part * lines : (part + 1) * lines].reshape(-1), me * rows, rows)

    table_total = small_out[0, 2 * lines : used].reshape(bucket_count, heads)
    return (
        output, input_grad, query, key, value_w, project, gate_w, up_w, down,
        own_gain(0), own_gain(1), table_total,
    )


def solution(mesh):
    rows = P(None, ("shard", "ctx"), None)
    weight = P(("shard", "ctx"), "tp")
    gain = P(("shard", "ctx"))
    table = P(None, "tp")
    return jax.shard_map(
        shards,
        mesh=mesh,
        in_specs=(rows, rows, P(None, "shard"), P("ctx", None)) + (weight,) * 7 + (gain, gain, table),
        out_specs=(rows, rows) + (weight,) * 7 + (gain, gain, table),
        check_vma=False,
    )
```

time: 2200 us -> 663 us (0.30)
  waiting for transfers between devices: 1560 us -> 16.6 us
  Pallas kernels: 0 us -> 449 us
  matrix products: 303 us -> 86.6 us
  blocking collectives: 161 us -> 0 us
  local copies, waits for them, and re-layouts: 90.7 us -> 49 us
    all_gather x18 -> x0, waiting for transfers between devices: 763 us -> none  [the longest x2 134 us: micro_step(): lax.all_gather(down_weight, ('shard', 'ctx'), axis=0, tiled=True)]
    reduce_scatter x11 -> x0, waiting for transfers between devices: 706 us -> none  [the longest x1 130 us: shards(): lax.psum_scatter(grad_sums[5], ('shard', 'ctx'), scatter_dimension=0, til...]
    pallas_call x0 -> x6, Pallas kernels: none -> 449 us  [the longest x1 165 us: scatter_gradients(): pl.pallas_call(functools.partial(scatter_kernel, shard_size, chunks, tens...]
    dot_general x60 -> x19, matrix products: 303 us -> 86.6 us  [dot(): lax.dot_general(a, b, (((left,), (right,)), ((), ())), preferred_element_...]
    while x2 -> x0, blocking collectives: 84.7 us -> none
    unnamed x1 -> x0, blocking collectives: 76.2 us -> none
    psum x6 -> x0, waiting for transfers between devices: 74.4 us -> none  [the longest x2 40 us: backward_pass(): lax.psum(times_transposed(grad_gate, gate_full) + times_transposed(grad_u...]
    while x226 -> x0, local copies, waits for them, and re-layouts: 31.9 us -> none
  transfers between devices with their start and end apart: 35 -> 13, of which waited for: 33 -> 3; matrix products, arithmetic and copies ran while one was open for 12% -> 12% of each run, Pallas kernels for 0% -> 64%
where the time goes in v1:
time: 663 us; the launch traced here: 657 us
  Pallas kernels  449 us (68%)
  matrix products  86.6 us (13%)
  local copies, waits for them, and re-layouts  49 us (7%)
  other arithmetic  39.4 us (6%)
  waiting for transfers between devices  16.6 us (3%)
  between operations  10 us (2%)
    pallas_call x1, Pallas kernels, scatter_gradients(): pl.pallas_call(functools.partial(scatter_kernel, shard_size, chunks, tens...  165 us
    pallas_call x1, Pallas kernels, gather_weights(): pl.pallas_call(functools.partial(gather_kernel, shard_size, chunks), out_...  142 us
    dot_general x19, matrix products, dot(): lax.dot_general(a, b, (((left,), (right,)), ((), ())), preferred_element_...  86.6 us
    pallas_call x1, Pallas kernels, attention_backward(): pl.pallas_call(functools.partial(backward_kernel, blocks=blocks), grid=(p...  52.4 us
    pallas_call x1, Pallas kernels, bias_bands(): pl.pallas_call(bias_kernel, grid=(blocks, heads), in_specs=[pl.BlockSpec(...  40.2 us
    unnamed x144, local copies, waits for them, and re-layouts  32.4 us
    pallas_call x1, Pallas kernels, attention_forward(): pl.pallas_call(functools.partial(forward_kernel, blocks=blocks), grid=(pa...  26.1 us
    pallas_call x1, Pallas kernels, table_band(): pl.pallas_call(functools.partial(table_kernel, buckets=buckets), grid=(bl...  23.4 us
  transfers between devices with their start and end apart: 13, of which 3 were waited for; matrix products, arithmetic and copies ran while one was open for 12% of the time, Pallas kernels for 64%

profile of v1, /device:TPU:0, one launch (start us, length us, event | category | flops | bytes accessed | tf_op | source)
XLA Modules:
  0.0 657.0 jit_solution(18402900618291882322)
XLA Ops:
  0.7 1.4 fusion.72
  9.8 1.3 fusion.59
  12.0 2.9 collective-permute-start.2
  14.9 1.6 fusion.46
  23.3 142.1 %gather_weights.1 = bf16[4,2,2,64,6400]{4,3,2,1,0:T(8,128)(2,1)} custom-call(bf16[64,6400]{1,0:T(8,128)(2,1)} %copy-done.48), custom_call_target="tpu_custom_call" | custom-call | tf_op jit(solution)/shard_map/gather_weights/pallas_call | solution.py:386
  166.4 2.0 slice_convert_fusion
  171.6 1.6 copy.91
  173.8 40.2 %bias_bands.1 = (f32[8,8,128,384]{3,2,1,0:T(8,128)}, f32[8,8,384,128]{3,2,1,0:T(8,128)}) custom-call(s32[8,128,384]{2,1,0:T(8,128)} %bitcast.267, s32[8,384,128]{2,1,0:T(8,128)} %bitcast.239, f32[8,8,128]{2,1,0:T(8,128)} %broadcast_in_dim.110.table_ref), custom_call_target="tpu_custom_call" | custom-call | tf_op jit(solution)/shard_map/bias_bands/pallas_call | solution.py:43
  214.1 1.4 select_bitcast_fusion.9
  215.7 1.4 copy-done.25
  219.5 2.4 fusion.7
  222.1 1.3 copy-done.20
  223.4 6.3 convolution_convert_fusion.3.q_ref.k_ref.v_ref
  229.7 26.1 %attention_forward.1 = (bf16[1024,512]{1,0:T(8,128)(2,1)S(1)}, f32[4,2,1024]{2,1,0:T(2,128)S(1)}) custom-call(bf16[1024,1536]{1,0:T(8,128)(2,1)S(1)} %convolution_convert_fusion.3.q_ref.k_ref.v_ref, bf16[1024,1536]{1,0:T(8,128)(2,1)S(1)} %convolution_convert_fusion.3.q_ref.k_ref.v_ref, bf16[1024,1536]{1,0:T(8,128)(2,1)S(1)} %convolution_convert_fusion.3.q_ref.k_ref.v_ref, ...), custom_call_target="tpu_custom_call" | custom-call | tf_op jit(solution)/shard_map/attention_forward/pallas_call | solution.py:105
  255.8 2.9 fusion.53
  258.7 2.0 copy-done.38
  265.0 3.0 multiply_reduce_fusion.3
  268.0 1.3 copy-done.16
  271.0 8.5 %fusion.11 = f32[1024,1408]{1,0:T(8,128)} fusion(bf16[1024,1024]{1,0:T(8,128)(2,1)} %get-tuple-element.186, bf16[1024,6400]{1,0:T(8,128)(2,1)} %bitcast.255), kind=kOutput, calls=%fused_computation.30 | convolution fusion | flops 2952790016 | bytes 10747904 | tf_op jit(solution)/shard_map/dot_general | solution.py:585
  279.5 1.7 select_bitcast_fusion.7
  282.3 5.2 fusion.17
  287.5 12.3 %fusion.6 = (bf16[1024,1408]{1,0:T(8,128)(2,1)}, bf16[1024,1408]{1,0:T(8,128)(2,1)}, bf16[1024,1408]{1,0:T(8,128)(2,1)}) fusion(f32[1024,1408]{1,0:T(8,128)} %fusion.11, f32[1024,1408]{1,0:T(8,128)} %fusion.17, bf16[1024,1024]{1,0:T(8,128)(2,1)S(1)} %bitcast.285, bf16[1024,6400]{1,0:T(8,128)(2,1)S(1)} %bitcast.262), kind=kOutput, calls=%fused_computation.8 | convolution fusion | flops 2988834816 | bytes 25165824 | tf_op jit(solution)/shard_map/dot_general | solution.py:585
  299.8 5.4 fusion.13
  305.3 3.4 fusion.15
  308.7 5.3 fusion.38
  314.4 2.7 copy-done.43
  317.1 6.8 %convolution_convert_fusion.2 = bf16[1024,1408]{1,0:T(8,128)(2,1)} fusion(bf16[1024,1024]{1,0:T(8,128)(2,1)S(1)} %copy-done.43, bf16[1024,1408]{1,0:T(8,128)(2,1)} %get-tuple-element.146), kind=kOutput, calls=%fused_computation.27 | convolution fusion | flops 2954231808 | bytes 7864320 | tf_op jit(solution)/shard_map/dot_general | solution.py:585
  325.5 5.0 convolution_convert_fusion.1
  333.1 5.2 fusion.69
  340.0 7.6 %convolution_convert_fusion = bf16[1024,1408]{1,0:T(8,128)(2,1)} fusion(bf16[1024,1024]{1,0:T(8,128)(2,1)} %bitcast.286, bf16[1024,1408]{1,0:T(8,128)(2,1)} %get-tuple-element.145), kind=kOutput, calls=%fused_computation.25 | convolution fusion | flops 2954231808 | bytes 7864320 | tf_op jit(solution)/shard_map/dot_general | solution.py:585
  347.6 5.8 collective-permute-done.6
  356.6 52.4 %attention_backward.1 = (bf16[1024,512]{1,0:T(8,128)(2,1)S(1)}, bf16[1024,512]{1,0:T(8,128)(2,1)S(1)}, bf16[1024,512]{1,0:T(8,128)(2,1)S(1)}, bf16[8,8,384,128]{3,2,1,0:T(8,128)(2,1)S(1)}, f32[8,8,1024]{2,1,0:T(8,128)S(1)}) custom-call(bf16[1024,1536]{1,0:T(8,128)(2,1)S(1)} %convolution_convert_fusion.3.q_ref.k_ref.v_ref, ...), custom_call_target="tpu_custom_call" | custom-call | tf_op jit(solution)/shard_map/attention_backward/pallas_call | solution.py:197
  409.1 23.4 %table_band.1 = f32[512,128]{1,0:T(8,128)S(1)} custom-call(s32[8,384,128]{2,1,0:T(8,128)S(1)} %bitcast.240, bf16[8,8,384,128]{3,2,1,0:T(8,128)(2,1)S(1)} %get-tuple-element.60.gs_ref), custom_call_target="tpu_custom_call" | custom-call | tf_op jit(solution)/shard_map/table_band/pallas_call | solution.py:273
  433.9 2.6 fusion.48
  436.5 2.6 fusion.50
  439.1 2.5 add_add_fusion
  441.6 2.0 copy-done.22
  445.5 3.0 convolution_convert_fusion.7
  450.8 1.3 copy-done.23
  452.1 1.9 fusion.34
  454.0 1.9 fusion.33
  458.4 3.2 convolution_convert_fusion.5
  461.6 10.2 %collective-permute-done.11 = bf16[256,1024]{1,0:T(8,128)(2,1)} collective-permute-done((bf16[256,1024]{1,0:T(8,128)(2,1)}, bf16[256,1024]{1,0:T(8,128)(2,1)}, u32[]{:S(2)}, u32[]{:S(2)}) %collective-permute-start.11) | collective-permute-done | bytes 524320 | tf_op jit(solution)/shard_map/ppermute | solution.py:589
  475.7 1.5 select_bitcast_fusion.5
  477.4 1.5 copy.97
  478.9 165.3 %scatter_gradients.1 = (f32[64,1408]{1,0:T(8,128)S(1)}, f32[64,1408]{1,0:T(8,128)S(1)}, f32[64,1408]{1,0:T(8,128)S(1)}, f32[64,512]{1,0:T(8,128)S(1)}, f32[64,51...) custom-call(bf16[4,2,2,64,1408]{4,3,2,1,0:T(8,128)(2,1)} %bitcast.276, ...), custom_call_target="tpu_custom_call" | custom-call | tf_op jit(solution)/shard_map/scatter_gradients/pallas_call | solution.py:541
  647.4 1.7 select_bitcast_fusion.1
  649.4 2.3 copy.101
  (239 shorter events, 51.6 us)
Async XLA Ops:
  0.6 164.8 %copy-start = (s32[2,1]{0,1:T(1,128)S(1)}, s32[2,1]{0,1:T(1,128)}, u32[]{:S(2)}) copy-start(s32[2,1]{0,1:T(1,128)} %param.21) | copy-start | bytes 28
  12.0 158.3 %collective-permute-start.2 = (bf16[4,128,384]{2,1,0:T(8,128)(2,1)}, bf16[4,128,384]{2,1,0:T(8,128)(2,1)}, u32[]{:S(2)}, u32[]{:S(2)}) collective-permute-start(bf16[4,128,384]{2,1,0:T(8,128)(2,1)} %pad_maximum_fusion.7), channel_id=1, source_target_pairs={{0,2},{2,0},{1,3},{3,1},{4,6},{6,4},{5,7},{7,5},{8,10},{10,8},{9,1... | collective-permute-start | bytes 1179656 | tf_op jit(solution)/shard_map/ppermute | solution.py:589
  14.9 5.6 copy-start.49
  16.5 151.9 %collective-permute-start = (bf16[2,256,1024]{2,1,0:T(8,128)(2,1)S(1)}, bf16[2,256,1024]{2,1,0:T(8,128)(2,1)S(1)}, u32[]{:S(2)}, u32[]{:S(2)}) collective-permute-start(bf16[2,256,1024]{2,1,0:T(8,128)(2,1)S(1)} %fusion.46), channel_id=1, source_target_pairs={{0,2},{2,0},{1,3},{3,1},{4,6},{6,4},{5,7},{7,5},{8,10},{10,8},{9,1... | collective-permute-start | bytes 3145736 | tf_op jit(solution)/shard_map/ppermute | solution.py:589
  23.3 142.7 %copy-start.52 = (s32[4,2]{1,0:T(4,128)S(1)}, s32[4,2]{1,0:T(4,128)}, u32[]{:S(2)}) copy-start(s32[4,2]{1,0:T(4,128)} %constant.231) | copy-start | bytes 100
  23.3 142.7 %copy-start.53 = (s32[4,2]{1,0:T(4,128)S(1)}, s32[4,2]{1,0:T(4,128)}, u32[]{:S(2)}) copy-start(s32[4,2]{1,0:T(4,128)} %constant.229) | copy-start | bytes 100
  168.4 45.7 %collective-permute-start.1 = (bf16[2,256,1024]{2,1,0:T(8,128)(2,1)S(1)}, bf16[2,256,1024]{2,1,0:T(8,128)(2,1)}, u32[]{:S(2)}, u32[]{:S(2)}) collective-permute-start(bf16[2,256,1024]{2,1,0:T(8,128)(2,1)S(1)} %collective-permute-done), channel_id=1, source_target_pairs={{0,1},{1,0},{2,3},{3,2},{4,5},{5,4},{6,7},{7,6},{8,9},{9,8},{10,11... | collective-permute-start | bytes 3145736 | tf_op jit(solution)/shard_map/ppermute | solution.py:589
  219.5 2.6 copy-start.18
  219.5 3.9 copy-start.20
  223.4 6.3 copy-start.40
  255.8 2.9 copy-start.9
  258.7 3.7 copy-start.50
  258.7 3.7 copy-start.54
  261.9 3.1 collective-permute-start.3
  270.5 9.0 %collective-permute-start.4 = (bf16[2,256,1024]{2,1,0:T(8,128)(2,1)}, bf16[2,256,1024]{2,1,0:T(8,128)(2,1)}, u32[]{:S(2)}, u32[]{:S(2)}) collective-permute-start(bf16[2,256,1024]{2,1,0:T(8,128)(2,1)} %multiply_convert_fusion.2), channel_id=1, source_target_pairs={{0,1},{1,0},{2,3},{3,2},{4,5},{5,4},{6,7},{7,6},{8,9},{9,8},{10,11... | collective-permute-start | bytes 3145736 | tf_op jit(solution)/shard_map/ppermute | solution.py:589
  270.9 8.6 %copy-start.17 = (f32[2,256,1024]{2,1,0:T(8,128)S(1)}, f32[2,256,1024]{2,1,0:T(8,128)}, u32[]{:S(2)}) copy-start(f32[2,256,1024]{2,1,0:T(8,128)} %copy-done.16) | copy-start | bytes 6291460
  270.9 10.7 %slice-start = ((s8[13107200]{0:T(1024)(128)(4,1)}), s8[4194304]{0:T(1024)(128)(4,1)S(1)}, s32[]{:S(2)}) async-start(s8[13107200]{0:T(1024)(128)(4,1)} %bitcast.259), calls=%async_computation | async-start | bytes 8388608
  271.0 10.7 %slice-start.1 = ((s8[13107200]{0:T(1024)(128)(4,1)}), s8[4194304]{0:T(1024)(128)(4,1)S(1)}, s32[]{:S(2)}) async-start(s8[13107200]{0:T(1024)(128)(4,1)} %bitcast.259), calls=%async_computation.1 | async-start | bytes 8388608
  271.0 10.7 %slice-start.2 = ((s8[13107200]{0:T(1024)(128)(4,1)}), s8[4194304]{0:T(1024)(128)(4,1)S(1)}, s32[]{:S(2)}) async-start(s8[13107200]{0:T(1024)(128)(4,1)} %bitcast.259), calls=%async_computation.2 | async-start | bytes 8388608
  281.6 5.9 copy-start.44
  299.8 5.4 copy-start.58
  305.3 18.7 %copy-start.39 = (f32[1024,1024]{1,0:T(8,128)}, f32[1024,1024]{1,0:T(8,128)S(1)}, u32[]{:S(2)}) copy-start(f32[1024,1024]{1,0:T(8,128)S(1)} %fusion.13) | copy-start | bytes 12582916
  314.0 16.6 %copy-start.28 = (f32[1024,1024]{1,0:T(8,128)}, f32[1024,1024]{1,0:T(8,128)S(1)}, u32[]{:S(2)}) copy-start(f32[1024,1024]{1,0:T(8,128)S(1)} %fusion.38) | copy-start | bytes 12582916
  314.0 3.1 copy-start.43
  314.2 16.4 %collective-permute-start.8 = (bf16[2,256,1024]{2,1,0:T(8,128)(2,1)S(1)}, bf16[2,256,1024]{2,1,0:T(8,128)(2,1)S(1)}, u32[]{:S(2)}, u32[]{:S(2)}) collective-permute-start(bf16[2,256,1024]{2,1,0:T(8,128)(2,1)S(1)} %fusion.42), channel_id=1, source_target_pairs={{0,1},{1,0},{2,3},{3,2},{4,5},{5,4},{6,7},{7,6},{8,9},{9,8},{10,11... | collective-permute-start | bytes 3145736 | tf_op jit(solution)/shard_map/ppermute | solution.py:589
  317.1 7.2 %copy-start.57 = (bf16[1024,1408]{1,0:T(8,128)(2,1)S(1)}, bf16[1024,1408]{1,0:T(8,128)(2,1)}, u32[]{:S(2)}) copy-start(bf16[1024,1408]{1,0:T(8,128)(2,1)} %get-tuple-element.144) | copy-start | bytes 8650756
  324.1 7.3 %collective-permute-start.5 = (bf16[2,256,1024]{2,1,0:T(8,128)(2,1)S(1)}, bf16[2,256,1024]{2,1,0:T(8,128)(2,1)S(1)}, u32[]{:S(2)}, u32[]{:S(2)}) collective-permute-start(bf16[2,256,1024]{2,1,0:T(8,128)(2,1)S(1)} %fusion.43), channel_id=1, source_target_pairs={{0,1},{1,0},{2,3},{3,2},{4,5},{5,4},{6,7},{7,6},{8,9},{9,8},{10,11... | collective-permute-start | bytes 3145736 | tf_op jit(solution)/shard_map/ppermute | solution.py:589
  339.4 14.0 %collective-permute-start.6 = (bf16[256,1024]{1,0:T(8,128)(2,1)S(1)}, bf16[256,1024]{1,0:T(8,128)(2,1)S(1)}, u32[]{:S(2)}, u32[]{:S(2)}) collective-permute-start(bf16[256,1024]{1,0:T(8,128)(2,1)S(1)} %dynamic-slice_bitcast_fusion.1), channel_id=1, source_target_pairs={{0,2},{2,0},{1,3},{3,1},{4,6},{6,4},{5,7},{7,5},{8,10},{10,8},{9,1... | collective-permute-start | bytes 1572872 | tf_op jit(solution)/shard_map/ppermute | solution.py:589
  340.0 13.4 %copy-start.37 = (bf16[2,256,1024]{2,1,0:T(8,128)(2,1)S(1)}, bf16[2,256,1024]{2,1,0:T(8,128)(2,1)}, u32[]{:S(2)}) copy-start(bf16[2,256,1024]{2,1,0:T(8,128)(2,1)} %get-tuple-element.155) | copy-start | bytes 3145732
  340.0 14.7 %collective-permute-start.9 = (bf16[2,256,1024]{2,1,0:T(8,128)(2,1)S(1)}, bf16[2,256,1024]{2,1,0:T(8,128)(2,1)S(1)}, u32[]{:S(2)}, u32[]{:S(2)}) collective-permute-start(bf16[2,256,1024]{2,1,0:T(8,128)(2,1)S(1)} %get-tuple-element.138), channel_id=1, source_target_pairs={{0,1},{1,0},{2,3},{3,2},{4,5},{5,4},{6,7},{7,6},{8,9},{9,8},{10,11... | collective-permute-start | bytes 3145736 | tf_op jit(solution)/shard_map/ppermute | solution.py:589
  354.7 120.9 %collective-permute-start.7 = (bf16[2,256,1024]{2,1,0:T(8,128)(2,1)}, bf16[2,256,1024]{2,1,0:T(8,128)(2,1)}, u32[]{:S(2)}, u32[]{:S(2)}) collective-permute-start(bf16[2,256,1024]{2,1,0:T(8,128)(2,1)} %pad_maximum_fusion.5), channel_id=1, source_target_pairs={{0,1},{1,0},{2,3},{3,2},{4,5},{5,4},{6,7},{7,6},{8,9},{9,8},{10,11... | collective-permute-start | bytes 3145736 | tf_op jit(solution)/shard_map/ppermute | solution.py:589
  356.6 52.4 %copy-start.2 = (s32[2,4,128,384]{2,3,1,0:T(8,128)S(1)}, s32[2,4,128,384]{2,3,1,0:T(8,128)}, u32[]{:S(2)}) copy-start(s32[2,4,128,384]{2,3,1,0:T(8,128)} %copy.91) | copy-start | bytes 4718596
  409.0 23.4 %copy-start.3 = (bf16[1024,512]{1,0:T(8,128)(2,1)}, bf16[1024,512]{1,0:T(8,128)(2,1)S(1)}, u32[]{:S(2)}) copy-start(bf16[1024,512]{1,0:T(8,128)(2,1)S(1)} %get-tuple-element.59) | copy-start | bytes 3145732
  409.0 23.4 %copy-start.11 = (bf16[1024,512]{1,0:T(8,128)(2,1)}, bf16[1024,512]{1,0:T(8,128)(2,1)S(1)}, u32[]{:S(2)}) copy-start(bf16[1024,512]{1,0:T(8,128)(2,1)S(1)} %get-tuple-element.58) | copy-start | bytes 3145732
  409.0 23.4 %copy-start.13 = (bf16[1024,512]{1,0:T(8,128)(2,1)}, bf16[1024,512]{1,0:T(8,128)(2,1)S(1)}, u32[]{:S(2)}) copy-start(bf16[1024,512]{1,0:T(8,128)(2,1)S(1)} %get-tuple-element.57) | copy-start | bytes 3145732
  436.5 2.6 copy-start.4
  441.6 3.9 copy-start.10
  444.8 5.1 collective-permute-start.10
  445.5 3.1 copy-start.15
  445.5 3.1 copy-start.41
  448.6 3.5 copy-start.23
  449.9 4.1 copy-start.27
  457.7 14.2 %collective-permute-start.11 = (bf16[256,1024]{1,0:T(8,128)(2,1)}, bf16[256,1024]{1,0:T(8,128)(2,1)}, u32[]{:S(2)}, u32[]{:S(2)}) collective-permute-start(bf16[256,1024]{1,0:T(8,128)(2,1)} %dynamic-slice_bitcast_fusion), channel_id=1, source_target_pairs={{0,2},{2,0},{1,3},{3,1},{4,6},{6,4},{5,7},{7,5},{8,10},{10,8},{9,1... | collective-permute-start | bytes 1572872 | tf_op jit(solution)/shard_map/ppermute | solution.py:589
  458.4 13.5 %copy-start.36 = (bf16[2,256,1024]{2,1,0:T(8,128)(2,1)S(1)}, bf16[2,256,1024]{2,1,0:T(8,128)(2,1)}, u32[]{:S(2)}) copy-start(bf16[2,256,1024]{2,1,0:T(8,128)(2,1)} %copy-done.35) | copy-start | bytes 3145732
  461.6 12.8 %copy-start.42 = (bf16[1024,1024]{1,0:T(8,128)(2,1)S(1)}, bf16[1024,1024]{1,0:T(8,128)(2,1)}, u32[]{:S(2)}) copy-start(bf16[1024,1024]{1,0:T(8,128)(2,1)} %copy-done.40) | copy-start | bytes 6291460
  474.4 173.0 %collective-permute-start.12 = (bf16[2,256,1024]{2,1,0:T(8,128)(2,1)}, bf16[2,256,1024]{2,1,0:T(8,128)(2,1)}, u32[]{:S(2)}, u32[]{:S(2)}) collective-permute-start(bf16[2,256,1024]{2,1,0:T(8,128)(2,1)} %pad_maximum_fusion.6), channel_id=1, source_target_pairs={{0,1},{1,0},{2,3},{3,2},{4,5},{5,4},{6,7},{7,6},{8,9},{9,8},{10,11... | collective-permute-start | bytes 3145736 | tf_op jit(solution)/shard_map/ppermute | solution.py:589
  649.3 3.0 copy-start.6
  649.3 7.2 %copy-start.1 = (s32[2,1]{0,1:T(1,128)S(1)}, s32[2,1]{0,1:T(1,128)}, u32[]{:S(2)}) copy-start(s32[2,1]{0,1:T(1,128)} %param.21) | copy-start | bytes 28
  (28 other events, 44.3 us)
